TPU v7x, 32 devices: a whole 2x2x4 slice. The times are simulated.
32 devices in a mesh: blk: 8 (over y, x, core), expert: 4 (over z).
Axes of the slice: x: 2, y: 2, z: 4, core: 2. Of those that a mesh axis runs over, the one named last changes fastest.
Arguments:
- queries: bfloat16 [16, 72, 1024], P('expert', None, 'blk'), may hold values from -6 to 6
- keys: bfloat16 [16, 72, 1024], P('expert', None, 'blk'), may hold values from -6 to 6
- values: bfloat16 [16, 72, 1024], P('expert', None, 'blk'), may hold values from -24 to 24
- image_ids: int32 [256], P('blk'), may hold values from 0 to 2, as said below
- placement: int32 [256, 1], P('blk'), may hold values from 0 to 7; in each aligned block of 32 rows (0 to 31, 32 to 63, ...) at most 16 rows name the same one
- merge_gain: float32 [16, 288], P('expert'), may hold values from 0.1 to 1.9
- merge_weight: bfloat16 [16, 288, 2048], P('expert'), may hold values from -0.09375 to 0.09375
- text: bfloat16 [1024, 2048], P('blk'), may hold values from -6 to 6
- norm_gain: float32 [2048], replicated, may hold values from 0.1 to 1.9
- w_gate: bfloat16 [8, 3072, 2048], P('blk', 'expert'), may hold values from -0.125 to 0.125
- w_up: bfloat16 [8, 3072, 2048], P('blk', 'expert'), may hold values from -0.125 to 0.125
- w_down: bfloat16 [8, 3072, 2048], P('blk', 'expert'), may hold values from -0.15625 to 0.15625
- routes: int32 [1024, 8], P('blk'), may hold values from 0 to 127, all different within a row; in each aligned block of 128 rows (0 to 127, 128 to 255, ...) at most 10 rows name the same one
- route_gates: float32 [1024, 8], P('blk'), may hold values from 0.2 to 1
- cotangent: bfloat16 [1024, 2048], P('blk'), may hold values from -6 to 6
Outputs:
- llm_out: bfloat16 [1024, 2048], P('blk')
- attn_grad: float32 [16, 72, 1024], P('expert', None, 'blk')
Inputs may be any that keep to these rules, and one draw needn't show every extreme that they name: `image_ids`: three images in order: ids never fall along the sequence; image 0 holds from 16 to 31 merged rows and image 2 from 17 to 32. `placement`: among the 32 rows of one encoder index no shard is named more than 16 times. `routes`: each token names 8 different experts; among the 128 tokens of one shard no expert is named more than 10 times.
All inputs are finite; a program needn't handle non-finite values.
Results may differ from a plain program's by a relative error of at most 0.03.
Values may be sent and summed in bfloat16 or wider, within the bound.
No kernel may reach another device: no remote copies, remote signals or barrier semaphores. Data moves between devices by JAX's collectives and lax.ppermute only.
A program may use at most 64 MiB of HBM per device.

v0:
```python
import functools

import jax
import jax.numpy as jnp
from jax import lax
from jax.experimental import pallas as pl
from jax.experimental.pallas import tpu as pltpu
from jax.sharding import PartitionSpec as P

CAPX = 10
SLOTS = 16
SEND = 32
EPS = 1e-06
VMEM_BYTES = 24 * 1024 * 1024
F32 = jnp.float32
BF16 = jnp.bfloat16


def iota(shape, dim):
    return lax.broadcasted_iota(jnp.int32, shape, dim)


def dot(a, b):
    return jnp.dot(a.astype(BF16), b.astype(BF16), preferred_element_type=F32)


def dot_nt(a, b):
    return lax.dot_general(a, b, (((1,), (1,)), ((), ())), preferred_element_type=F32)


def dot_tn(a, b):
    return lax.dot_general(a, b, (((0,), (0,)), ((), ())), preferred_element_type=F32)


def three(value):
    first = value.astype(BF16).astype(F32)
    second = (value - first).astype(BF16).astype(F32)
    return first, second, value - first - second


def put_scalars(columns, rows):
    lane = iota((rows, 128), 1)
    out = jnp.zeros((rows, 128), F32)
    place = 0
    for column in columns:
        for piece in three(column):
            out = jnp.where(lane == place, piece, out)
            place += 1
    return out


def get_scalar(block, which):
    lane = iota(block.shape, 1)
    return jnp.sum(jnp.where(lane // 3 == which, block, 0.0), axis=1, keepdims=True)


def pack_kernel(*refs):
    far_refs, out_ref, near_refs, sems = refs[:5], refs[5], refs[6:11], refs[11]
    copies = [
        pltpu.make_async_copy(far, near, sems.at[i])
        for i, (far, near) in enumerate(zip(far_refs, near_refs))
    ]
    for copy in copies:
        copy.start()
    for copy in copies:
        copy.wait()
    keys_ref, values_ref, images_ref, placement_ref, routes_ref = near_refs
    rows = images_ref.shape[1]
    patches = keys_ref.shape[1]
    repeat = (iota((rows, patches), 0) == iota((rows, patches), 1) // 4).astype(F32)
    keep = (iota((rows, patches), 0) == iota((rows, patches), 1)).astype(F32)
    patch_ids = dot(images_ref[...].astype(F32), repeat)
    dest = dot(placement_ref[...].astype(F32), keep)
    line = iota((8, patches), 0)
    rest = jnp.where(line == 0, patch_ids, jnp.where(line == 1, dest, 0.0))
    parts = [keys_ref[...], values_ref[...], routes_ref[...], rest]
    out_ref[...] = jnp.concatenate([part.astype(F32) for part in parts], axis=0).astype(BF16)


def hold_kernel(*refs):
    count = (len(refs) - 1) // 2
    copies = []
    sems = refs[-1]
    for i in range(count):
        far_ref, near_ref = refs[i], refs[count + i]
        chunk = far_ref.shape[0] // sems.shape[1]
        for j in range(sems.shape[1]):
            mine = pl.ds(j * chunk, chunk)
            copies.append(pltpu.make_async_copy(far_ref.at[mine], near_ref.at[mine], sems.at[i, j]))
            copies[-1].start()
    for copy in copies:
        copy.wait()


def plan_kernel(*refs, blocks, groups, merged_rows, row_share):
    near_refs = refs[:blocks]
    routes_ref, gates_ref, text_ref, gain_ref, cot_ref, _ = refs[blocks : blocks + 6]
    slots_ref, placed_ref, comb_ref, send_ref = refs[blocks + 6 :]
    tokens = text_ref.shape[0]
    share = merged_rows // row_share
    rows = blocks * merged_rows
    me, expert_index = lax.axis_index("blk"), lax.axis_index("expert")
    member = expert_index // groups
    meta = [ref[...].astype(F32) for ref in near_refs]
    mine = (2 * me + member).astype(F32)
    hits = [jnp.sum((part[:8] == mine).astype(F32), axis=0, keepdims=True) for part in meta]
    hit = jnp.concatenate(hits, axis=0)
    dest = jnp.concatenate([part[9:10] for part in meta], axis=0)
    before = (iota((tokens, tokens), 0) < iota((tokens, tokens), 1)).astype(BF16)
    rank = dot(hit, before)

    def row_of(col):
        inner = col % merged_rows
        return ((inner // row_share) ^ expert_index) * row_share + inner % row_share

    def place_of(col):
        return ((col // merged_rows) ^ me) * merged_rows + row_of(col)

    spread = (iota((128, rows), 0) == row_of(iota((128, rows), 1))).astype(F32)
    own_block = iota((blocks, rows), 1) // merged_rows == iota((blocks, rows), 0)
    dest_row = jnp.sum(jnp.where(own_block, dot(dest, spread), 0.0), axis=0, keepdims=True)
    dest_row = dest_row.astype(jnp.int32) ^ me
    dest_hit = (iota((blocks, rows), 0) == dest_row).astype(F32)
    rows_before = place_of(iota((rows, rows), 0)) < place_of(iota((rows, rows), 1))
    earlier = dot(dest_hit, rows_before.astype(F32))
    slot = jnp.sum(dest_hit * earlier, axis=0, keepdims=True).astype(jnp.int32)
    at_token = (iota((tokens, rows), 0) == slot).astype(F32)
    row_hit = jnp.sum(dest_hit * dot(hit, at_token), axis=0, keepdims=True)
    row_rank = jnp.sum(dest_hit * dot(rank, at_token), axis=0, keepdims=True).astype(jnp.int32)
    slot_id = (dest_row ^ me) * SLOTS + row_rank
    slot_count = slots_ref.shape[0]
    chosen = (iota((slot_count, rows), 0) == slot_id) & (row_hit > 0.5)
    slots_ref[...] = chosen.astype(F32).astype(BF16)
    placed = jnp.where(dest_row == 0, at_token, 0.0).astype(BF16)
    placed_ref[...] = placed

    pair_of = 2 * iota((blocks, tokens), 0) + member
    out_hit = jnp.zeros((blocks, tokens), F32)
    out_gate = jnp.zeros((blocks, tokens), F32)
    for k in range(routes_ref.shape[0]):
        same = pair_of == routes_ref[k : k + 1, :]
        out_hit = out_hit + same.astype(F32)
        out_gate = out_gate + jnp.where(same, gates_ref[k : k + 1, :], 0.0)
    out_rank = dot(out_hit, before)

    def expand(stride):
        count = blocks * stride
        pick = (iota((count, blocks), 0) // stride == iota((count, blocks), 1)).astype(BF16)
        gate = sum(dot(pick, piece) for piece in three(out_gate))
        return dot(pick, out_hit), dot(pick, out_rank).astype(jnp.int32), gate

    hits, ranks, gates = expand(SLOTS)
    live = jnp.where(ranks == iota(hits.shape, 0) % SLOTS, hits, 0.0)
    weight = live * gates
    high = weight.astype(BF16).astype(F32)
    part = tokens // share
    col = iota((tokens, tokens), 1)
    turned = (col // part * 0).astype(jnp.int32)
    for place, k in enumerate(halving_order(share)):
        turned = jnp.where(col // part == place, k, turned)
    turned = (iota((tokens, tokens), 0) == (turned ^ expert_index) * part + col % part)
    turned = turned.astype(F32)
    comb_ref[0] = dot(high, turned).astype(BF16)
    comb_ref[1] = dot(weight - high, turned).astype(BF16)

    hits, ranks, gates = expand(SEND)
    place = iota(hits.shape, 0) % SEND
    input_pick = jnp.where((place < CAPX) & (ranks == place), hits, 0.0)
    back_pick = jnp.where((place >= CAPX) & (place < 2 * CAPX) & (ranks == place - CAPX), hits, 0.0)
    back_gate = jnp.sum(back_pick * gates, axis=1, keepdims=True)
    send_rows = blocks * SEND
    source = iota((send_rows, rows), 0)
    kept = source % SEND - 2 * CAPX
    wanted = ((source // SEND) ^ me) * merged_rows + kept
    row_pick = (kept >= 0) & (kept < row_share) & (iota((send_rows, rows), 1) == wanted)
    cot_pick = dot_nt(row_pick.astype(F32).astype(BF16), placed)
    cot_row = iota((send_rows, 1), 0) % SEND >= 2 * CAPX
    factor = jnp.where(cot_row, 1.0, back_gate)
    text = text_ref[...].astype(F32)
    scale = lax.rsqrt(jnp.mean(text * text, axis=1, keepdims=True) + EPS)
    h_rows = (text * scale * gain_ref[...]).astype(BF16)
    send = dot(input_pick, h_rows) + factor * dot(back_pick + cot_pick, cot_ref[...])
    send_ref[...] = send.astype(BF16)


def flat_gain(gain_ref):
    return jnp.concatenate([gain_ref[h : h + 1] for h in range(gain_ref.shape[0])], axis=1)


def attend_kernel(*refs, blocks, share, row_share):
    query_ref, gain_ref, weight_ref = refs[:3]
    near_refs = refs[3 : 3 + blocks]
    merged_ref, *message_refs = refs[3 + blocks :]
    heads, size, patches = query_ref.shape
    rows, features = merged_ref.shape
    width = weight_ref.shape[1]
    depth = heads * size
    near = [ref[...].astype(F32) for ref in near_refs]
    key_ids = jnp.concatenate([part[2 * depth + 8 : 2 * depth + 9] for part in near], axis=1)
    eye = iota((patches, patches), 0) == iota((patches, patches), 1)
    own_ids = jnp.sum(jnp.where(eye, key_ids[:, :patches], 0.0), axis=1, keepdims=True)
    same = own_ids == key_ids
    spread = jnp.zeros((patches, features), F32)
    place_row, place_col = iota((size, features), 0), iota((size, features), 1)
    for head in range(heads):
        first = head * size
        keys = jnp.concatenate([part[first : first + size] for part in near], axis=1)
        first = depth + head * size
        values = jnp.concatenate([part[first : first + size] for part in near], axis=1)
        query = query_ref[head].astype(F32).T.astype(BF16)
        scores = dot(query, keys) * (size**-0.5)
        scores = jnp.where(same, scores, -1e30)
        weights = jnp.exp(scores - jnp.max(scores, axis=1, keepdims=True))
        total = jnp.sum(weights, axis=1, keepdims=True)
        attn = dot_nt(weights.astype(BF16), values.astype(BF16)) / total
        place = (place_col % size == place_row) & (place_col // (4 * size) == head)
        spread = spread + dot(attn, place.astype(F32))
    spot = iota((patches, features), 1) // size % 4 == iota((patches, features), 0) % 4
    line = iota((rows, patches), 0)
    line = ((line // row_share) ^ lax.axis_index("expert")) * row_share + line % row_share
    fold = (iota((rows, patches), 1) // 4 == line).astype(F32)
    merged = dot(fold, jnp.where(spot, spread, 0.0))
    merged_ref[...] = merged.astype(BF16)
    local_mean = jnp.sum(merged, axis=1, keepdims=True) / features
    centered = merged - local_mean
    squares = jnp.sum(centered * centered, axis=1, keepdims=True)
    gain = flat_gain(gain_ref)
    gain_high = gain.astype(BF16).astype(F32)
    extra = iota((8, features), 0)
    gain_rows = jnp.where(extra == 0, gain_high, jnp.where(extra == 1, gain - gain_high, 0.0))
    left = jnp.concatenate([centered * gain, gain_rows], axis=0)
    product = dot(left, weight_ref[...])
    gain_sum = product[rows : rows + 1] + product[rows + 1 : rows + 2]
    piece = width // row_share
    pieces = [gain_sum[:, j * piece : (j + 1) * piece] for j in range(row_share)]
    pieces = jnp.concatenate(pieces, axis=0).astype(BF16)
    scalars = put_scalars([local_mean, squares], rows).astype(BF16)
    for k in range(share):
        mine = slice(k * row_share, (k + 1) * row_share)
        message_refs[k][:, :width] = product[mine].astype(BF16)
        message_refs[k][:, width : width + piece] = pieces
        message_refs[k][:, width + piece :] = scalars[mine]


def merge_kernel(*refs, width, features):
    *message_refs, out_ref = refs
    share, row_share = len(message_refs), out_ref.shape[0]
    piece = width // row_share
    parts = [ref[...].astype(F32) for ref in message_refs]
    scalars = [part[:, width + piece :] for part in parts]
    means = [get_scalar(block, 0) for block in scalars]
    squares = [get_scalar(block, 1) for block in scalars]
    mean = sum(means) / share
    spread = sum(q + features * (m - mean) * (m - mean) for q, m in zip(squares, means))
    inv_std = lax.rsqrt(spread / (share * features) + EPS)
    total = jnp.zeros((row_share, width), F32)
    for part, local in zip(parts, means):
        tail = part[:, width : width + piece]
        gain_sum = jnp.concatenate([tail[j : j + 1] for j in range(row_share)], axis=1)
        total = total + part[:, :width] + (local - mean) * gain_sum
    out_ref[:, :width] = (total * inv_std).astype(BF16)
    out_ref[:, width:] = put_scalars([mean, inv_std], row_share).astype(BF16)


def stack_kernel(*refs):
    *part_refs, out_ref = refs
    out_ref[...] = stacked(part_refs)


def stacked(part_refs):
    return jnp.concatenate([ref[...].astype(F32) for ref in part_refs], axis=0).astype(BF16)


def slot_pick(slot_count, send_rows, shift):
    row, col = iota((slot_count, send_rows), 0), iota((slot_count, send_rows), 1)
    place = row % SLOTS
    pick = (col == row // SLOTS * SEND + place + shift) & (place < CAPX)
    return pick.astype(F32)


def forward_kernel(*refs, blocks):
    slots_ref, gain_ref, gate_ref, up_ref, down_ref, early_ref = refs[:6]
    vision_refs = refs[6 : 6 + blocks]
    gate_out, up_out, down_out, h_ref, sum_ref = refs[6 + blocks :]
    hidden, width = gate_ref.shape
    slot_count = slots_ref.shape[0]
    chosen = slots_ref[...]
    is_vision = jnp.sum(chosen.astype(F32), axis=1, keepdims=True) > 0.5
    vision = jnp.concatenate([ref[:, :width] for ref in vision_refs], axis=0)
    inputs = dot(chosen, vision)
    scale = lax.rsqrt(jnp.mean(inputs * inputs, axis=1, keepdims=True) + EPS)
    normed = inputs * scale * gain_ref[...]
    early = early_ref[...]
    text_rows = dot(slot_pick(slot_count, early.shape[0], 0), early)
    h_ref[...] = jnp.where(is_vision, normed, text_rows).astype(BF16)
    tile = tile_of(hidden)
    for i in range(hidden // tile):
        mine = slice(i * tile, (i + 1) * tile)
        gate_pre = dot_nt(h_ref[...], gate_ref[mine])
        up_proj = dot_nt(h_ref[...], up_ref[mine])
        gate_out[:, mine] = gate_pre
        up_out[:, mine] = up_proj
        activated = gate_pre * jax.nn.sigmoid(gate_pre) * up_proj
        product = dot(activated, down_ref[mine])
        sum_ref[...] = product if i == 0 else sum_ref[...] + product
    down_out[...] = sum_ref[...].astype(BF16)


def backward_kernel(
    slots_ref, early_ref, gate_in, up_in, gate_ref, up_ref, down_ref, even_ref, odd_ref,
    back_ref, sum_ref, *, blocks,
):
    hidden = gate_ref.shape[0]
    slot_count = slots_ref.shape[0]
    early = early_ref[...]
    back_ref[...] = dot(slot_pick(slot_count, early.shape[0], CAPX), early).astype(BF16)
    tile = tile_of(hidden)
    for i in range(hidden // tile):
        mine = slice(i * tile, (i + 1) * tile)
        act_grad = dot_nt(back_ref[...], down_ref[mine])
        gate_pre, up_proj = gate_in[:, mine], up_in[:, mine]
        sigmoid = jax.nn.sigmoid(gate_pre)
        gate_grad = act_grad * up_proj * sigmoid * (1.0 + gate_pre * (1.0 - sigmoid))
        up_grad = act_grad * gate_pre * sigmoid
        product = dot(gate_grad, gate_ref[mine]) + dot(up_grad, up_ref[mine])
        sum_ref[...] = product if i == 0 else sum_ref[...] + product
    grads = dot_tn(slots_ref[...], sum_ref[...].astype(BF16)).astype(BF16)
    rows = grads.shape[0] // blocks
    for k in range(blocks):
        to_ref = odd_ref if k % 2 else even_ref
        to_ref[k // 2 * rows : (k // 2 + 1) * rows] = grads[k * rows : (k + 1) * rows]


def tile_of(hidden):
    return 256 if hidden % 256 == 0 else hidden


def halving_order(share):
    order = [0]
    step = share // 2
    while step:
        order = order + [k + step for k in order]
        step //= 2
    return [sum(1 << j for j in range(share.bit_length() - 1) if k >> j & 1) for k in order]


def pair_sum_kernel(own_ref, sibling_ref, *out_refs):
    rows = out_refs[0].shape[0]
    for k, out_ref in enumerate(out_refs):
        mine = slice(k * rows, (k + 1) * rows)
        out_ref[...] = (own_ref[mine].astype(F32) + sibling_ref[mine].astype(F32)).astype(BF16)


def total_of(part_refs):
    total = part_refs[0][...].astype(F32)
    for ref in part_refs[1:]:
        total = total + ref[...].astype(F32)
    return total


def chip_sum_kernel(*refs, count):
    out_refs = refs[count:]
    total = total_of(refs[:count])
    rows = out_refs[0].shape[0]
    for k, out_ref in enumerate(out_refs):
        out_ref[...] = total[k * rows : (k + 1) * rows].astype(BF16)


def combine_kernel(comb_ref, rows_ref, keep_ref, send_ref):
    rows = rows_ref[...]
    total = dot_tn(comb_ref[0], rows) + dot_tn(comb_ref[1], rows)
    half = keep_ref.shape[0]
    keep_ref[...] = total[:half]
    send_ref[...] = total[half:].astype(BF16)


def halve_kernel(own_ref, arrived_ref, keep_ref, send_ref):
    total = own_ref[...] + arrived_ref[...].astype(F32)
    half = keep_ref.shape[0]
    keep_ref[...] = total[:half]
    send_ref[...] = total[half:].astype(BF16)


def finish_kernel(placed_ref, text_ref, own_ref, arrived_ref, *refs):
    *vision_refs, out_ref = refs
    count, width = out_ref.shape
    tokens = placed_ref.shape[0]
    first = lax.axis_index("expert") * count
    pick = iota((count, tokens), 1) == iota((count, tokens), 0) + first
    pick = pick.astype(F32)
    placed = dot(pick, placed_ref[...])
    is_vision = jnp.sum(placed, axis=1, keepdims=True) > 0.5
    vision = jnp.concatenate([ref[:, :width] for ref in vision_refs], axis=0)
    inputs = jnp.where(is_vision, dot(placed, vision), dot(pick, text_ref[...]))
    out_ref[...] = (inputs + own_ref[...] + arrived_ref[...].astype(F32)).astype(BF16)


def lay_kernel(*refs):
    *part_refs, out_ref = refs
    count = part_refs[0].shape[0]
    for k, ref in enumerate(part_refs):
        first = pl.multiple_of((lax.axis_index("expert") ^ k) * count, count)
        out_ref[pl.ds(first, count), :] = ref[...]


def norm_grad_kernel(own_ref, gain_ref, early_ref, *refs):
    *part_refs, out_ref = refs
    row_share, width = out_ref.shape
    hidden = total_of(part_refs)
    early = early_ref[...]
    send_rows = early.shape[0]
    pick = iota((row_share, send_rows), 1) % SEND == iota((row_share, send_rows), 0) + 2 * CAPX
    cotangent = dot(pick.astype(F32), early)
    inputs = own_ref[:, :width].astype(F32)
    scale = lax.rsqrt(jnp.mean(inputs * inputs, axis=1, keepdims=True) + EPS)
    pulled = hidden * gain_ref[...]
    cross = jnp.mean(pulled * inputs, axis=1, keepdims=True)
    grad = cotangent + scale * pulled - inputs * (scale * scale * scale) * cross
    out_ref[...] = grad.astype(BF16)


def merge_grad_kernel(*refs):
    gain_ref, merged_ref, scalar_ref, weight_ref, *part_refs = refs[:-2]
    out_ref, sums_ref = refs[-2:]
    width = weight_ref.shape[1]
    normed_grad = dot_nt(stacked(part_refs), weight_ref[...]) * flat_gain(gain_ref)
    out_ref[...] = normed_grad
    scalars = scalar_ref[:, width:].astype(F32)
    normed = (merged_ref[...].astype(F32) - get_scalar(scalars, 0)) * get_scalar(scalars, 1)
    first = jnp.sum(normed_grad, axis=1, keepdims=True)
    second = jnp.sum(normed_grad * normed, axis=1, keepdims=True)
    lane = iota(sums_ref.shape, 1)
    sums_ref[...] = jnp.where(lane == 0, first, jnp.where(lane == 1, second, 0.0))


def unfold_kernel(grad_ref, merged_ref, scalar_ref, *refs, size):
    *sums_refs, out_ref = refs
    rows, features = grad_ref.shape
    depth, patches = out_ref.shape
    share = len(sums_refs)
    row_share = rows // share
    sums = sums_refs[0][...]
    for k in range(1, share):
        theirs = [sums_refs[k][(j ^ k) * row_share : ((j ^ k) + 1) * row_share] for j in range(share)]
        sums = sums + jnp.concatenate(theirs, axis=0)
    sums = sums / (share * features)
    lane = iota(sums.shape, 1)
    grad_mean = jnp.sum(jnp.where(lane == 0, sums, 0.0), axis=1, keepdims=True)
    cross_mean = jnp.sum(jnp.where(lane == 1, sums, 0.0), axis=1, keepdims=True)
    scalars = scalar_ref[:, scalar_ref.shape[1] - 128 :].astype(F32)
    inv_std = get_scalar(scalars, 1)
    normed = (merged_ref[...].astype(F32) - get_scalar(scalars, 0)) * inv_std
    grad = inv_std * (grad_ref[...] - grad_mean - normed * cross_mean)
    high = grad.astype(BF16)
    low = (grad - high.astype(F32)).astype(BF16)
    line = iota((patches, rows), 1)
    line = ((line // row_share) ^ lax.axis_index("expert")) * row_share + line % row_share
    unfold = (iota((patches, rows), 0) // 4 == line).astype(F32)
    spot = iota((patches, features), 1) // size % 4 == iota((patches, features), 0) % 4
    row, col = iota((depth, features), 0), iota((depth, features), 1)
    place = (col // (4 * size) == row // size) & (col % size == row % size)
    place = place.astype(F32).astype(BF16)
    out = jnp.zeros((depth, patches), F32)
    for piece in (high, low):
        wide = jnp.where(spot, dot(unfold, piece), 0.0).astype(BF16)
        out = out + dot_nt(place, wide)
    out_ref[...] = out


def whole(memory_space=pltpu.VMEM):
    return pl.BlockSpec(memory_space=memory_space)


def run(kernel, outs, *args, far=(), scratch=(), cost=1.0, name=None):
    specs = [whole()] * len(args)
    for place in far:
        specs[place] = whole(pltpu.HBM)
    return pl.pallas_call(
        kernel,
        out_shape=outs,
        in_specs=specs,
        out_specs=jax.tree.map(lambda _: whole(), outs),
        scratch_shapes=scratch,
        compiler_params=pltpu.CompilerParams(vmem_limit_bytes=VMEM_BYTES),
        cost_estimate=microseconds(cost),
        name=name,
    )(*args)


def microseconds(time):
    return pl.CostEstimate(flops=0, transcendentals=0, bytes_accessed=int(time * 3e6))


def shape(dims, dtype=BF16):
    return jax.ShapeDtypeStruct(dims, dtype)


def swap(value, axis, step):
    count = lax.axis_size(axis)
    return lax.ppermute(value, axis, [(i, i ^ step) for i in range(count)])


def trade(parts, axis):
    return [parts[0]] + [swap(parts[k], axis, k) for k in range(1, len(parts))]


def spread_out(value, axis):
    return trade([value] * lax.axis_size(axis), axis)


def gather_blocks(value):
    near = {0: value}
    for k in range(2, lax.axis_size("blk"), 2):
        near[k] = swap(value, "blk", k)
    for k in list(near):
        near[k + 1] = swap(near[k], "blk", 1)
    return [near[k] for k in sorted(near)]


def hold(arrays, after=None, name=None):
    if after is not None:
        *arrays, _ = lax.optimization_barrier((*arrays, after))
    chunks = 3 if arrays[0].shape[0] % 48 == 0 else 1
    return run(
        hold_kernel, [shape(array.shape) for array in arrays], *arrays,
        far=tuple(range(len(arrays))),
        scratch=[pltpu.SemaphoreType.DMA((len(arrays), chunks))],
        cost=sum(array.size for array in arrays) / 1e6, name=name,
    )


def send_all(value, axis):
    return lax.all_to_all(value, axis, split_axis=0, concat_axis=0, tiled=True)


def body(
    queries, keys, values, image_ids, placement, merge_gain, merge_weight, text, norm_gain,
    w_gate, w_up, w_down, routes, route_gates, cotangent,
):
    blocks = lax.axis_size("blk")
    share = lax.axis_size("expert")
    heads, size, patches = queries.shape
    depth = heads * size
    rows = image_ids.shape[0]
    row_share = rows // share
    tokens, width = text.shape
    part = tokens // share
    all_rows = blocks * rows
    features = heads * 4 * size
    hidden = w_gate.shape[1]
    slot_count = blocks * SLOTS
    groups = share // 2
    routes_t, gates_t, gain_row = routes.T, route_gates.T, norm_gain[None]

    small = [
        keys.reshape(depth, patches), values.reshape(depth, patches),
        image_ids[None], placement.reshape(1, rows), routes_t,
    ]
    local = run(
        pack_kernel, shape((2 * depth + 16, patches)), *small, far=range(5),
        scratch=[pltpu.VMEM(array.shape, array.dtype) for array in small]
        + [pltpu.SemaphoreType.DMA((5,))],
        name="pack",
    )
    near = gather_blocks(local)
    weight_flat = merge_weight.reshape(features, width)
    (weight_near,) = hold([weight_flat], name="hold_merge")

    message_width = width + width // row_share + 128
    merged, *message = run(
        functools.partial(attend_kernel, blocks=blocks, share=share, row_share=row_share),
        [shape((rows, features))] + [shape((row_share, message_width))] * share,
        queries, merge_gain, weight_near, *near, cost=4.0, name="attend",
    )

    def fixed(*dims):
        return pl.BlockSpec(dims, lambda i: (0,) * len(dims))

    meta_spec = pl.BlockSpec((16, patches), lambda i: (2 * depth // 16, 0))
    plan_outs = [
        shape((slot_count, all_rows)), shape((tokens, all_rows)), shape((2, slot_count, tokens)),
        shape((blocks * SEND, width)),
    ]
    slots, placed, comb, send = pl.pallas_call(
        functools.partial(
            plan_kernel, blocks=blocks, groups=groups, merged_rows=rows, row_share=row_share
        ),
        grid=(1,),
        in_specs=[meta_spec] * blocks
        + [
            fixed(*routes_t.shape), fixed(*gates_t.shape), fixed(tokens, width), fixed(1, width),
            fixed(tokens, width), whole(pl.ANY),
        ],
        out_specs=[fixed(*out.shape) for out in plan_outs],
        out_shape=plan_outs,
        compiler_params=pltpu.CompilerParams(vmem_limit_bytes=VMEM_BYTES),
        cost_estimate=microseconds(2.0),
        name="plan",
    )(*near, routes_t, gates_t, text, gain_row, cotangent, merged)
    early = send_all(send.reshape(blocks, SEND, width), "blk").reshape(blocks * SEND, width)

    message = trade(message, "expert")
    own = run(
        functools.partial(merge_kernel, width=width, features=features),
        shape((row_share, width + 128)), *message, cost=0.2, name="merge",
    )
    block_rows = run(
        stack_kernel, shape((rows, width + 128)), *spread_out(own, "expert"), cost=0.2, name="stack"
    )
    vision = gather_blocks(block_rows)
    gate_near, up_near, down_near = hold(
        [w_gate[0], w_up[0], w_down[0]], after=own, name="hold_experts"
    )

    gate_pre, up_proj, down = run(
        functools.partial(forward_kernel, blocks=blocks),
        [
            shape((slot_count, hidden), F32), shape((slot_count, hidden), F32),
            shape((slot_count, width)),
        ],
        slots, gain_row, gate_near, up_near, down_near, early, *vision,
        scratch=[pltpu.VMEM((slot_count, width), BF16), pltpu.VMEM((slot_count, width), F32)],
        cost=5.0, name="forward",
    )
    returned = send_all(down.reshape(blocks, SLOTS, width), "blk").reshape(slot_count, width)
    even, odd = run(
        functools.partial(backward_kernel, blocks=blocks),
        [shape((all_rows // 2, width))] * 2,
        slots, early, gate_pre, up_proj, gate_near, up_near, down_near,
        scratch=[pltpu.VMEM((slot_count, width), BF16), pltpu.VMEM((slot_count, width), F32)],
        cost=5.0, name="backward",
    )
    grads = run(
        pair_sum_kernel, [shape((rows, width))] * (blocks // 2), even, swap(odd, "blk", 1),
        cost=0.2, name="pair_sum",
    )
    grads = [grads[0]] + [swap(grads[k], "blk", 2 * k) for k in range(1, blocks // 2)]
    grads = run(
        functools.partial(chip_sum_kernel, count=blocks // 2),
        [shape((row_share, width))] * share, *grads, cost=0.2, name="chip_sum",
    )
    grads = trade(grads, "expert")
    vision_grad = run(
        norm_grad_kernel, shape((row_share, width)), own, gain_row, early, *grads,
        cost=0.3, name="norm_grad",
    )
    (weight_again,) = hold([weight_flat], after=down, name="hold_merge_again")
    normed_grad, sums = run(
        merge_grad_kernel,
        [shape((rows, features), F32), shape((rows, 128), F32)],
        merge_gain, merged, block_rows, weight_again, *spread_out(vision_grad, "expert"),
        cost=2.5, name="merge_grad",
    )
    sums = spread_out(sums, "expert")

    count = tokens // 2
    kept, sent = run(
        combine_kernel, [shape((count, width), F32), shape((count, width))], comb, returned,
        cost=0.5, name="combine",
    )
    step = 1
    while count > part:
        count //= 2
        kept, sent = run(
            halve_kernel, [shape((count, width), F32), shape((count, width))],
            kept, swap(sent, "expert", step), cost=0.3, name="halve",
        )
        step *= 2
    finished = run(
        finish_kernel, shape((part, width)),
        placed, text, kept, swap(sent, "expert", step), *vision, cost=1.0, name="finish",
    )
    laid = {0: finished}
    while step:
        laid.update({k + step: swap(laid[k], "expert", step) for k in list(laid)})
        step //= 2
    llm_out = run(
        lay_kernel, shape((tokens, width)), *[laid[k] for k in sorted(laid)], cost=1.0, name="lay"
    )
    attn_grad = run(
        functools.partial(unfold_kernel, size=size), shape((depth, patches), F32),
        normed_grad, merged, block_rows, *sums, cost=2.0, name="unfold",
    )
    return llm_out, attn_grad.reshape(heads, size, patches)


def solution(mesh):
    return jax.shard_map(
        body,
        mesh=mesh,
        in_specs=(
            P("expert", None, "blk"),
            P("expert", None, "blk"),
            P("expert", None, "blk"),
            P("blk"),
            P("blk", None),
            P("expert", None),
            P("expert", None, None),
            P("blk", None),
            P(),
            P("blk", "expert", None),
            P("blk", "expert", None),
            P("blk", "expert", None),
            P("blk", None),
            P("blk", None),
            P("blk", None),
        ),
        out_specs=(P("blk", None), P("expert", None, "blk")),
        check_vma=False,
    )
```

profile of v0, /device:TPU:0, one launch (start us, length us, event | category | flops | bytes accessed | tf_op | source)
XLA Modules:
  0.0 149.6 jit_solution(16755797256969995356)
XLA Ops:
  4.8 4.0 %collective-permute-start.5 = (bf16[592,128]{1,0:T(8,128)(2,1)S(1)}, bf16[592,128]{1,0:T(8,128)(2,1)S(1)}, u32[]{:S(2)}, u32[]{:S(2)}) collective-permute-start(bf16[592,128]{1,0:T(8,128)(2,1)S(1)} %pack.1.refs_3_.refs_0_), channel_id=1, source_target_pairs={{0,24},{4,28},{8,16},{12,20},{16,8},{20,12},{24,0},{28,4},{1,25},{... | collective-permute-start | bytes 454664 | tf_op jit(solution)/shard_map/ppermute | solution.py:500
  9.4 3.8 %collective-permute-done.5.refs_9_.refs_6_ = bf16[592,128]{1,0:T(8,128)(2,1)S(1)} collective-permute-done((bf16[592,128]{1,0:T(8,128)(2,1)S(1)}, bf16[592,128]{1,0:T(8,128)(2,1)S(1)}, u32[]{:S(2)}, u32[]{:S(2)}) %collective-permute-start.5) | collective-permute-done | bytes 151584 | tf_op jit(solution)/shard_map/ppermute | solution.py:500
  13.2 2.7 %collective-permute-done.3.refs_7_.refs_4_ = bf16[592,128]{1,0:T(8,128)(2,1)S(1)} collective-permute-done((bf16[592,128]{1,0:T(8,128)(2,1)S(1)}, bf16[592,128]{1,0:T(8,128)(2,1)S(1)}, u32[]{:S(2)}, u32[]{:S(2)}) %collective-permute-start.3) | collective-permute-done | bytes 151584 | tf_op jit(solution)/shard_map/ppermute | solution.py:500
  16.4 2.3 %copy-done = bf16[4,288,2048]{2,1,0:T(8,128)(2,1)S(1)} copy-done((bf16[4,288,2048]{2,1,0:T(8,128)(2,1)S(1)}, bf16[4,288,2048]{2,1,0:T(8,128)(2,1)}, u32[]{:S(2)}) %copy-start) | copy-done | bytes 4718616
  19.7 3.4 %attend.1 = (bf16[32,1152]{1,0:T(8,128)(2,1)S(1)}, bf16[8,2432]{1,0:T(8,128)(2,1)S(1)}, bf16[8,2432]{1,0:T(8,128)(2,1)S(1)}, bf16[8,2432]{1,0:T(8,128)(2,1)S(1)}, bf16[8,2432]{1,0:T(8,128)(2,1)S(1)}) custom-call(bf16[4,72,128]{2,1,0:T(8,128)(2,1)S(1)} %copy-done.26, f32[4,288]{1,0:T(4,128)S(1)} %copy-done.27, bf16[1152,2048]{1,0:T(8,128)(2,1)S(1)} %hold_merge.1.refs_2_, ...), custom_call_target="tpu_custom_call" | custom-call | bytes 12000000 | tf_op jit(solution)/shard_map/attend/pallas_call | solution.py:478
  23.1 2.4 %plan.1 = (bf16[128,256]{1,0:T(8,128)(2,1)S(1)}, bf16[128,256]{1,0:T(8,128)(2,1)S(1)}, bf16[2,128,128]{2,1,0:T(8,128)(2,1)S(1)}, bf16[256,2048]{1,0:T(8,128)(2,1)}) custom-call(bf16[592,128]{1,0:T(8,128)(2,1)S(1)} %pack.1.refs_3_.refs_0_, bf16[592,128]{1,0:T(8,128)(2,1)S(1)} %collective-permute-done.refs_4_.refs_1_, ...), custom_call_target="tpu_custom_call" | custom-call | bytes 6000000 | tf_op jit(solution)/shard_map/plan/pallas_call | solution.py:584
  25.6 3.6 %all-to-all-start = ((bf16[8,32,2048]{2,1,0:T(8,128)(2,1)}), bf16[8,32,2048]{2,1,0:T(8,128)(2,1)S(1)}, u32[]{:S(2)}, u32[]{:S(2)}) async-start(bf16[8,32,2048]{2,1,0:T(8,128)(2,1)} %bitcast.11), calls=%async_computation | async-start | bytes 2097152 | tf_op jit(solution)/shard_map/all_to_all | solution.py:533
  31.0 2.6 %collective-permute-start.8 = (bf16[8,2432]{1,0:T(8,128)(2,1)S(1)}, bf16[8,2432]{1,0:T(8,128)(2,1)S(1)}, u32[]{:S(2)}, u32[]{:S(2)}) collective-permute-start(bf16[8,2432]{1,0:T(8,128)(2,1)S(1)} %get-tuple-element.43), channel_id=1, source_target_pairs={{0,2},{1,3},{2,0},{3,1},{4,6},{5,7},{6,4},{7,5},{8,10},{9,11},{10,... | collective-permute-start | bytes 116744 | tf_op jit(solution)/shard_map/ppermute | solution.py:500
  33.6 2.9 %collective-permute-done.8.refs_2_ = bf16[8,2432]{1,0:T(8,128)(2,1)S(1)} collective-permute-done((bf16[8,2432]{1,0:T(8,128)(2,1)S(1)}, bf16[8,2432]{1,0:T(8,128)(2,1)S(1)}, u32[]{:S(2)}, u32[]{:S(2)}) %collective-permute-start.8) | collective-permute-done | bytes 38944 | tf_op jit(solution)/shard_map/ppermute | solution.py:500
  36.5 2.8 %collective-permute-done.9.refs_3_ = bf16[8,2432]{1,0:T(8,128)(2,1)S(1)} collective-permute-done((bf16[8,2432]{1,0:T(8,128)(2,1)S(1)}, bf16[8,2432]{1,0:T(8,128)(2,1)S(1)}, u32[]{:S(2)}, u32[]{:S(2)}) %collective-permute-start.9) | collective-permute-done | bytes 38944 | tf_op jit(solution)/shard_map/ppermute | solution.py:500
  40.2 3.7 %collective-permute-start.10 = (bf16[8,2176]{1,0:T(8,128)(2,1)S(1)}, bf16[8,2176]{1,0:T(8,128)(2,1)S(1)}, u32[]{:S(2)}, u32[]{:S(2)}) collective-permute-start(bf16[8,2176]{1,0:T(8,128)(2,1)S(1)} %merge.1.refs_0_.own_ref), channel_id=1, source_target_pairs={{0,1},{1,0},{2,3},{3,2},{4,5},{5,4},{6,7},{7,6},{8,9},{9,8},{10,11... | collective-permute-start | bytes 104456 | tf_op jit(solution)/shard_map/ppermute | solution.py:500
  45.9 2.8 %collective-permute-start.18 = (bf16[32,2176]{1,0:T(8,128)(2,1)S(1)}, bf16[32,2176]{1,0:T(8,128)(2,1)S(1)}, u32[]{:S(2)}, u32[]{:S(2)}) collective-permute-start(bf16[32,2176]{1,0:T(8,128)(2,1)S(1)} %stack.1.refs_6_.refs_0_.refs_2_.scalar_ref), channel_id=1, source_target_pairs={{0,24},{4,28},{8,16},{12,20},{16,8},{20,12},{24,0},{28,4},{1,25},{... | collective-permute-start | bytes 417800 | tf_op jit(solution)/shard_map/ppermute | solution.py:500
  49.5 2.8 %collective-permute-done.18.refs_12_.refs_6_ = bf16[32,2176]{1,0:T(8,128)(2,1)S(1)} collective-permute-done((bf16[32,2176]{1,0:T(8,128)(2,1)S(1)}, bf16[32,2176]{1,0:T(8,128)(2,1)S(1)}, u32[]{:S(2)}, u32[]{:S(2)}) %collective-permute-start.18) | collective-permute-done | bytes 139296 | tf_op jit(solution)/shard_map/ppermute | solution.py:500
  54.3 1.9 %copy-done.11 = bf16[1,768,2048]{2,1,0:T(8,128)(2,1)S(1)} copy-done((bf16[1,768,2048]{2,1,0:T(8,128)(2,1)S(1)}, bf16[1,768,2048]{2,1,0:T(8,128)(2,1)}, u32[]{:S(2)}) %copy-start.11) | copy-done | bytes 3145752
  56.2 1.9 %copy-done.12 = bf16[1,768,2048]{2,1,0:T(8,128)(2,1)S(1)} copy-done((bf16[1,768,2048]{2,1,0:T(8,128)(2,1)S(1)}, bf16[1,768,2048]{2,1,0:T(8,128)(2,1)}, u32[]{:S(2)}) %copy-start.12) | copy-done | bytes 3145752
  58.1 1.9 %copy-done.13 = bf16[1,768,2048]{2,1,0:T(8,128)(2,1)S(1)} copy-done((bf16[1,768,2048]{2,1,0:T(8,128)(2,1)S(1)}, bf16[1,768,2048]{2,1,0:T(8,128)(2,1)}, u32[]{:S(2)}) %copy-start.13) | copy-done | bytes 3145752
  67.7 1.9 %copy-done.6 = bf16[768,2048]{1,0:T(8,128)(2,1)S(1)} copy-done((bf16[768,2048]{1,0:T(8,128)(2,1)S(1)}, bf16[768,2048]{1,0:T(8,128)(2,1)}, u32[]{:S(2)}) %copy-start.6) | copy-done | bytes 3145752
  69.6 1.9 %copy-done.9 = bf16[768,2048]{1,0:T(8,128)(2,1)S(1)} copy-done((bf16[768,2048]{1,0:T(8,128)(2,1)S(1)}, bf16[768,2048]{1,0:T(8,128)(2,1)}, u32[]{:S(2)}) %copy-start.9) | copy-done | bytes 3145752
  71.5 3.3 %forward.1 = (f32[128,768]{1,0:T(8,128)S(1)}, f32[128,768]{1,0:T(8,128)S(1)}, bf16[128,2048]{1,0:T(8,128)(2,1)S(1)}) custom-call(bf16[128,256]{1,0:T(8,128)(2,1)S(1)} %get-tuple-element.40.refs_0_.slots_ref, f32[1,2048]{1,0:T(1,128)S(1)} %bitcast.27, bf16[768,2048]{1,0:T(8,128)(2,1)S(1)} %copy-done.3, bf16[768,2048]{1,0:T(8,128)(2,1)S(1)} %copy-done.6, ...), custom_call_target="tpu_custom_call" | custom-call | bytes 15000000 | tf_op jit(solution)/shard_map/forward/pallas_call | solution.py:478
  77.1 3.7 %all-to-all-start.1 = ((bf16[8,16,2048]{2,1,0:T(8,128)(2,1)}), bf16[8,16,2048]{2,1,0:T(8,128)(2,1)S(1)}, u32[]{:S(2)}, u32[]{:S(2)}) async-start(bf16[8,16,2048]{2,1,0:T(8,128)(2,1)} %bitcast.25), calls=%async_computation.1 | async-start | bytes 1048576 | tf_op jit(solution)/shard_map/all_to_all | solution.py:533
  82.7 1.9 %copy-done.7 = bf16[768,2048]{1,0:T(8,128)(2,1)S(1)} copy-done((bf16[768,2048]{1,0:T(8,128)(2,1)S(1)}, bf16[768,2048]{1,0:T(8,128)(2,1)}, u32[]{:S(2)}) %copy-start.7) | copy-done | bytes 3145752
  88.4 3.8 %backward.1 = (bf16[128,2048]{1,0:T(8,128)(2,1)S(1)}, bf16[128,2048]{1,0:T(8,128)(2,1)}) custom-call(bf16[128,256]{1,0:T(8,128)(2,1)S(1)} %get-tuple-element.40.refs_0_.slots_ref, bf16[256,2048]{1,0:T(8,128)(2,1)S(1)} %bitcast.19, f32[128,768]{1,0:T(8,128)S(1)} %copy-done.20, f32[128,768]{1,0:T(8,128)S(1)} %copy-done.22, bf16[768,2048]{1,0:T(8,128)(2,1)S(1)} %copy-done.4, ...), custom_call_target="tpu_custom_call" | custom-call | bytes 15000000 | tf_op jit(solution)/shard_map/backward/pallas_call | solution.py:478
  93.9 2.1 %collective-permute-start.20 = (bf16[64,2048]{1,0:T(8,128)(2,1)S(1)}, bf16[64,2048]{1,0:T(8,128)(2,1)S(1)}, u32[]{:S(2)}, u32[]{:S(2)}) collective-permute-start(bf16[64,2048]{1,0:T(8,128)(2,1)S(1)} %get-tuple-element.54), channel_id=1, source_target_pairs={{0,1},{1,0},{2,3},{3,2},{4,5},{5,4},{6,7},{7,6},{8,9},{9,8},{10,11... | collective-permute-start | bytes 786440 | tf_op jit(solution)/shard_map/ppermute | solution.py:500
  96.1 6.5 %collective-permute-done.20.arrived_ref = bf16[64,2048]{1,0:T(8,128)(2,1)S(1)} collective-permute-done((bf16[64,2048]{1,0:T(8,128)(2,1)S(1)}, bf16[64,2048]{1,0:T(8,128)(2,1)S(1)}, u32[]{:S(2)}, u32[]{:S(2)}) %collective-permute-start.20) | collective-permute-done | bytes 262176 | tf_op jit(solution)/shard_map/ppermute | solution.py:500
  103.7 7.6 %collective-permute-done.21.arrived_ref = bf16[32,2048]{1,0:T(8,128)(2,1)S(1)} collective-permute-done((bf16[32,2048]{1,0:T(8,128)(2,1)S(1)}, bf16[32,2048]{1,0:T(8,128)(2,1)S(1)}, u32[]{:S(2)}, u32[]{:S(2)}) %collective-permute-start.21) | collective-permute-done | bytes 131104 | tf_op jit(solution)/shard_map/ppermute | solution.py:500
  113.1 2.1 %collective-permute-start.26 = (bf16[32,2048]{1,0:T(8,128)(2,1)S(1)}, bf16[32,2048]{1,0:T(8,128)(2,1)S(1)}, u32[]{:S(2)}, u32[]{:S(2)}) collective-permute-start(bf16[32,2048]{1,0:T(8,128)(2,1)S(1)} %get-tuple-element.63), channel_id=1, source_target_pairs={{0,8},{4,12},{8,0},{12,4},{16,24},{20,28},{24,16},{28,20},{1,9},{5... | collective-permute-start | bytes 393224 | tf_op jit(solution)/shard_map/ppermute | solution.py:500
  116.7 2.2 %collective-permute-start.22 = (bf16[32,2048]{1,0:T(8,128)(2,1)S(1)}, bf16[32,2048]{1,0:T(8,128)(2,1)S(1)}, u32[]{:S(2)}, u32[]{:S(2)}) collective-permute-start(bf16[32,2048]{1,0:T(8,128)(2,1)S(1)} %finish.1.refs_0_), channel_id=1, source_target_pairs={{0,1},{1,0},{2,3},{3,2},{4,5},{5,4},{6,7},{7,6},{8,9},{9,8},{10,11... | collective-permute-start | bytes 393224 | tf_op jit(solution)/shard_map/ppermute | solution.py:500
  120.1 2.7 %collective-permute-done.27.refs_2_ = bf16[32,2048]{1,0:T(8,128)(2,1)S(1)} collective-permute-done((bf16[32,2048]{1,0:T(8,128)(2,1)S(1)}, bf16[32,2048]{1,0:T(8,128)(2,1)S(1)}, u32[]{:S(2)}, u32[]{:S(2)}) %collective-permute-start.27) | collective-permute-done | bytes 131104 | tf_op jit(solution)/shard_map/ppermute | solution.py:500
  122.9 2.4 %collective-permute-start.29 = (bf16[8,2048]{1,0:T(8,128)(2,1)S(1)}, bf16[8,2048]{1,0:T(8,128)(2,1)S(1)}, u32[]{:S(2)}, u32[]{:S(2)}) collective-permute-start(bf16[8,2048]{1,0:T(8,128)(2,1)S(1)} %get-tuple-element.67), channel_id=1, source_target_pairs={{0,1},{1,0},{2,3},{3,2},{4,5},{5,4},{6,7},{7,6},{8,9},{9,8},{10,11... | collective-permute-start | bytes 98312 | tf_op jit(solution)/shard_map/ppermute | solution.py:500
  127.7 2.4 %collective-permute-done.30.refs_2_ = bf16[8,2048]{1,0:T(8,128)(2,1)S(1)} collective-permute-done((bf16[8,2048]{1,0:T(8,128)(2,1)S(1)}, bf16[8,2048]{1,0:T(8,128)(2,1)S(1)}, u32[]{:S(2)}, u32[]{:S(2)}) %collective-permute-start.30) | collective-permute-done | bytes 32800 | tf_op jit(solution)/shard_map/ppermute | solution.py:500
  133.7 2.6 %collective-permute-start.32 = (bf16[8,2048]{1,0:T(8,128)(2,1)S(1)}, bf16[8,2048]{1,0:T(8,128)(2,1)S(1)}, u32[]{:S(2)}, u32[]{:S(2)}) collective-permute-start(bf16[8,2048]{1,0:T(8,128)(2,1)S(1)} %norm_grad.1.refs_4_), channel_id=1, source_target_pairs={{0,1},{1,0},{2,3},{3,2},{4,5},{5,4},{6,7},{7,6},{8,9},{9,8},{10,11... | collective-permute-start | bytes 98312 | tf_op jit(solution)/shard_map/ppermute | solution.py:500
  136.3 2.3 %copy-done.1 = bf16[4,288,2048]{2,1,0:T(8,128)(2,1)S(1)} copy-done((bf16[4,288,2048]{2,1,0:T(8,128)(2,1)S(1)}, bf16[4,288,2048]{2,1,0:T(8,128)(2,1)}, u32[]{:S(2)}) %copy-start.1) | copy-done | bytes 4718616
  (133 shorter events, 53.7 us)
Async XLA Ops:
  4.8 8.4 %collective-permute-start.5 = (bf16[592,128]{1,0:T(8,128)(2,1)S(1)}, bf16[592,128]{1,0:T(8,128)(2,1)S(1)}, u32[]{:S(2)}, u32[]{:S(2)}) collective-permute-start(bf16[592,128]{1,0:T(8,128)(2,1)S(1)} %pack.1.refs_3_.refs_0_), channel_id=1, source_target_pairs={{0,24},{4,28},{8,16},{12,20},{16,8},{20,12},{24,0},{28,4},{1,25},{... | collective-permute-start | bytes 454664 | tf_op jit(solution)/shard_map/ppermute | solution.py:500
  8.7 7.2 %collective-permute-start.3 = (bf16[592,128]{1,0:T(8,128)(2,1)S(1)}, bf16[592,128]{1,0:T(8,128)(2,1)S(1)}, u32[]{:S(2)}, u32[]{:S(2)}) collective-permute-start(bf16[592,128]{1,0:T(8,128)(2,1)S(1)} %pack.1.refs_3_.refs_0_), channel_id=1, source_target_pairs={{0,16},{4,20},{8,24},{12,28},{16,0},{20,4},{24,8},{28,12},{1,17},{... | collective-permute-start | bytes 454664 | tf_op jit(solution)/shard_map/ppermute | solution.py:500
  9.2 7.0 %collective-permute-start.1 = (bf16[592,128]{1,0:T(8,128)(2,1)S(1)}, bf16[592,128]{1,0:T(8,128)(2,1)S(1)}, u32[]{:S(2)}, u32[]{:S(2)}) collective-permute-start(bf16[592,128]{1,0:T(8,128)(2,1)S(1)} %pack.1.refs_3_.refs_0_), channel_id=1, source_target_pairs={{0,8},{4,12},{8,0},{12,4},{16,24},{20,28},{24,16},{28,20},{1,9},{5... | collective-permute-start | bytes 454664 | tf_op jit(solution)/shard_map/ppermute | solution.py:500
  9.4 9.8 %collective-permute-start = (bf16[592,128]{1,0:T(8,128)(2,1)S(1)}, bf16[592,128]{1,0:T(8,128)(2,1)S(1)}, u32[]{:S(2)}, u32[]{:S(2)}) collective-permute-start(bf16[592,128]{1,0:T(8,128)(2,1)S(1)} %pack.1.refs_3_.refs_0_), channel_id=1, source_target_pairs={{0,4},{4,0},{8,12},{12,8},{16,20},{20,16},{24,28},{28,24},{1,5},{5... | collective-permute-start | bytes 454664 | tf_op jit(solution)/shard_map/ppermute | solution.py:500
  13.2 6.0 %collective-permute-start.6 = (bf16[592,128]{1,0:T(8,128)(2,1)S(1)}, bf16[592,128]{1,0:T(8,128)(2,1)S(1)}, u32[]{:S(2)}, u32[]{:S(2)}) collective-permute-start(bf16[592,128]{1,0:T(8,128)(2,1)S(1)} %collective-permute-done.5.refs_9_.refs_6_), channel_id=1, source_target_pairs={{0,4},{4,0},{8,12},{12,8},{16,20},{20,16},{24,28},{28,24},{1,5},{5... | collective-permute-start | bytes 454664 | tf_op jit(solution)/shard_map/ppermute | solution.py:500
  25.6 40.2 %all-to-all-start = ((bf16[8,32,2048]{2,1,0:T(8,128)(2,1)}), bf16[8,32,2048]{2,1,0:T(8,128)(2,1)S(1)}, u32[]{:S(2)}, u32[]{:S(2)}) async-start(bf16[8,32,2048]{2,1,0:T(8,128)(2,1)} %bitcast.11), calls=%async_computation | async-start | bytes 2097152 | tf_op jit(solution)/shard_map/all_to_all | solution.py:533
  31.0 5.5 %collective-permute-start.8 = (bf16[8,2432]{1,0:T(8,128)(2,1)S(1)}, bf16[8,2432]{1,0:T(8,128)(2,1)S(1)}, u32[]{:S(2)}, u32[]{:S(2)}) collective-permute-start(bf16[8,2432]{1,0:T(8,128)(2,1)S(1)} %get-tuple-element.43), channel_id=1, source_target_pairs={{0,2},{1,3},{2,0},{3,1},{4,6},{5,7},{6,4},{7,5},{8,10},{9,11},{10,... | collective-permute-start | bytes 116744 | tf_op jit(solution)/shard_map/ppermute | solution.py:500
  33.6 5.8 %collective-permute-start.9 = (bf16[8,2432]{1,0:T(8,128)(2,1)S(1)}, bf16[8,2432]{1,0:T(8,128)(2,1)S(1)}, u32[]{:S(2)}, u32[]{:S(2)}) collective-permute-start(bf16[8,2432]{1,0:T(8,128)(2,1)S(1)} %get-tuple-element.44), channel_id=1, source_target_pairs={{0,3},{1,2},{2,1},{3,0},{4,7},{5,6},{6,5},{7,4},{8,11},{9,10},{10,... | collective-permute-start | bytes 116744 | tf_op jit(solution)/shard_map/ppermute | solution.py:500
  39.5 5.9 %collective-permute-start.12 = (bf16[8,2176]{1,0:T(8,128)(2,1)S(1)}, bf16[8,2176]{1,0:T(8,128)(2,1)S(1)}, u32[]{:S(2)}, u32[]{:S(2)}) collective-permute-start(bf16[8,2176]{1,0:T(8,128)(2,1)S(1)} %merge.1.refs_0_.own_ref), channel_id=1, source_target_pairs={{0,3},{1,2},{2,1},{3,0},{4,7},{5,6},{6,5},{7,4},{8,11},{9,10},{10,... | collective-permute-start | bytes 104456 | tf_op jit(solution)/shard_map/ppermute | solution.py:500
  40.2 5.7 %collective-permute-start.11 = (bf16[8,2176]{1,0:T(8,128)(2,1)S(1)}, bf16[8,2176]{1,0:T(8,128)(2,1)S(1)}, u32[]{:S(2)}, u32[]{:S(2)}) collective-permute-start(bf16[8,2176]{1,0:T(8,128)(2,1)S(1)} %merge.1.refs_0_.own_ref), channel_id=1, source_target_pairs={{0,2},{1,3},{2,0},{3,1},{4,6},{5,7},{6,4},{7,5},{8,10},{9,11},{10,... | collective-permute-start | bytes 104456 | tf_op jit(solution)/shard_map/ppermute | solution.py:500
  40.2 5.7 %collective-permute-start.10 = (bf16[8,2176]{1,0:T(8,128)(2,1)S(1)}, bf16[8,2176]{1,0:T(8,128)(2,1)S(1)}, u32[]{:S(2)}, u32[]{:S(2)}) collective-permute-start(bf16[8,2176]{1,0:T(8,128)(2,1)S(1)} %merge.1.refs_0_.own_ref), channel_id=1, source_target_pairs={{0,1},{1,0},{2,3},{3,2},{4,5},{5,4},{6,7},{7,6},{8,9},{9,8},{10,11... | collective-permute-start | bytes 104456 | tf_op jit(solution)/shard_map/ppermute | solution.py:500
  45.9 6.4 %collective-permute-start.18 = (bf16[32,2176]{1,0:T(8,128)(2,1)S(1)}, bf16[32,2176]{1,0:T(8,128)(2,1)S(1)}, u32[]{:S(2)}, u32[]{:S(2)}) collective-permute-start(bf16[32,2176]{1,0:T(8,128)(2,1)S(1)} %stack.1.refs_6_.refs_0_.refs_2_.scalar_ref), channel_id=1, source_target_pairs={{0,24},{4,28},{8,16},{12,20},{16,8},{20,12},{24,0},{28,4},{1,25},{... | collective-permute-start | bytes 417800 | tf_op jit(solution)/shard_map/ppermute | solution.py:500
  48.7 5.1 %collective-permute-start.16 = (bf16[32,2176]{1,0:T(8,128)(2,1)S(1)}, bf16[32,2176]{1,0:T(8,128)(2,1)S(1)}, u32[]{:S(2)}, u32[]{:S(2)}) collective-permute-start(bf16[32,2176]{1,0:T(8,128)(2,1)S(1)} %stack.1.refs_6_.refs_0_.refs_2_.scalar_ref), channel_id=1, source_target_pairs={{0,16},{4,20},{8,24},{12,28},{16,0},{20,4},{24,8},{28,12},{1,17},{... | collective-permute-start | bytes 417800 | tf_op jit(solution)/shard_map/ppermute | solution.py:500
  49.5 16.3 %collective-permute-start.13 = (bf16[32,2176]{1,0:T(8,128)(2,1)S(1)}, bf16[32,2176]{1,0:T(8,128)(2,1)S(1)}, u32[]{:S(2)}, u32[]{:S(2)}) collective-permute-start(bf16[32,2176]{1,0:T(8,128)(2,1)S(1)} %stack.1.refs_6_.refs_0_.refs_2_.scalar_ref), channel_id=1, source_target_pairs={{0,4},{4,0},{8,12},{12,8},{16,20},{20,16},{24,28},{28,24},{1,5},{5... | collective-permute-start | bytes 417800 | tf_op jit(solution)/shard_map/ppermute | solution.py:500
  52.3 13.5 %collective-permute-start.19 = (bf16[32,2176]{1,0:T(8,128)(2,1)S(1)}, bf16[32,2176]{1,0:T(8,128)(2,1)S(1)}, u32[]{:S(2)}, u32[]{:S(2)}) collective-permute-start(bf16[32,2176]{1,0:T(8,128)(2,1)S(1)} %collective-permute-done.18.refs_12_.refs_6_), channel_id=1, source_target_pairs={{0,4},{4,0},{8,12},{12,8},{16,20},{20,16},{24,28},{28,24},{1,5},{5... | collective-permute-start | bytes 417800 | tf_op jit(solution)/shard_map/ppermute | solution.py:500
  53.8 12.0 %collective-permute-start.17 = (bf16[32,2176]{1,0:T(8,128)(2,1)S(1)}, bf16[32,2176]{1,0:T(8,128)(2,1)S(1)}, u32[]{:S(2)}, u32[]{:S(2)}) collective-permute-start(bf16[32,2176]{1,0:T(8,128)(2,1)S(1)} %collective-permute-done.16.refs_10_.refs_4_), channel_id=1, source_target_pairs={{0,4},{4,0},{8,12},{12,8},{16,20},{20,16},{24,28},{28,24},{1,5},{5... | collective-permute-start | bytes 417800 | tf_op jit(solution)/shard_map/ppermute | solution.py:500
  54.3 11.5 %collective-permute-start.15 = (bf16[32,2176]{1,0:T(8,128)(2,1)S(1)}, bf16[32,2176]{1,0:T(8,128)(2,1)S(1)}, u32[]{:S(2)}, u32[]{:S(2)}) collective-permute-start(bf16[32,2176]{1,0:T(8,128)(2,1)S(1)} %collective-permute-done.14.refs_8_.refs_2_), channel_id=1, source_target_pairs={{0,4},{4,0},{8,12},{12,8},{16,20},{20,16},{24,28},{28,24},{1,5},{5... | collective-permute-start | bytes 417800 | tf_op jit(solution)/shard_map/ppermute | solution.py:500
  77.1 16.4 %all-to-all-start.1 = ((bf16[8,16,2048]{2,1,0:T(8,128)(2,1)}), bf16[8,16,2048]{2,1,0:T(8,128)(2,1)S(1)}, u32[]{:S(2)}, u32[]{:S(2)}) async-start(bf16[8,16,2048]{2,1,0:T(8,128)(2,1)} %bitcast.25), calls=%async_computation.1 | async-start | bytes 1048576 | tf_op jit(solution)/shard_map/all_to_all | solution.py:533
  93.0 18.9 %collective-permute-start.25 = (bf16[128,2048]{1,0:T(8,128)(2,1)}, bf16[128,2048]{1,0:T(8,128)(2,1)}, u32[]{:S(2)}, u32[]{:S(2)}) collective-permute-start(bf16[128,2048]{1,0:T(8,128)(2,1)} %get-tuple-element.61), channel_id=1, source_target_pairs={{0,4},{4,0},{8,12},{12,8},{16,20},{20,16},{24,28},{28,24},{1,5},{5... | collective-permute-start | bytes 1572872 | tf_op jit(solution)/shard_map/ppermute | solution.py:500
  93.9 8.6 %collective-permute-start.20 = (bf16[64,2048]{1,0:T(8,128)(2,1)S(1)}, bf16[64,2048]{1,0:T(8,128)(2,1)S(1)}, u32[]{:S(2)}, u32[]{:S(2)}) collective-permute-start(bf16[64,2048]{1,0:T(8,128)(2,1)S(1)} %get-tuple-element.54), channel_id=1, source_target_pairs={{0,1},{1,0},{2,3},{3,2},{4,5},{5,4},{6,7},{7,6},{8,9},{9,8},{10,11... | collective-permute-start | bytes 786440 | tf_op jit(solution)/shard_map/ppermute | solution.py:500
  102.6 8.7 %collective-permute-start.21 = (bf16[32,2048]{1,0:T(8,128)(2,1)S(1)}, bf16[32,2048]{1,0:T(8,128)(2,1)S(1)}, u32[]{:S(2)}, u32[]{:S(2)}) collective-permute-start(bf16[32,2048]{1,0:T(8,128)(2,1)S(1)} %get-tuple-element.56), channel_id=1, source_target_pairs={{0,2},{1,3},{2,0},{3,1},{4,6},{5,7},{6,4},{7,5},{8,10},{9,11},{10,... | collective-permute-start | bytes 393224 | tf_op jit(solution)/shard_map/ppermute | solution.py:500
  111.8 8.3 %collective-permute-start.23 = (bf16[32,2048]{1,0:T(8,128)(2,1)S(1)}, bf16[32,2048]{1,0:T(8,128)(2,1)S(1)}, u32[]{:S(2)}, u32[]{:S(2)}) collective-permute-start(bf16[32,2048]{1,0:T(8,128)(2,1)S(1)} %finish.1.refs_0_), channel_id=1, source_target_pairs={{0,2},{1,3},{2,0},{3,1},{4,6},{5,7},{6,4},{7,5},{8,10},{9,11},{10,... | collective-permute-start | bytes 393224 | tf_op jit(solution)/shard_map/ppermute | solution.py:500
  113.1 7.1 %collective-permute-start.26 = (bf16[32,2048]{1,0:T(8,128)(2,1)S(1)}, bf16[32,2048]{1,0:T(8,128)(2,1)S(1)}, u32[]{:S(2)}, u32[]{:S(2)}) collective-permute-start(bf16[32,2048]{1,0:T(8,128)(2,1)S(1)} %get-tuple-element.63), channel_id=1, source_target_pairs={{0,8},{4,12},{8,0},{12,4},{16,24},{20,28},{24,16},{28,20},{1,9},{5... | collective-permute-start | bytes 393224 | tf_op jit(solution)/shard_map/ppermute | solution.py:500
  115.1 7.7 %collective-permute-start.27 = (bf16[32,2048]{1,0:T(8,128)(2,1)S(1)}, bf16[32,2048]{1,0:T(8,128)(2,1)S(1)}, u32[]{:S(2)}, u32[]{:S(2)}) collective-permute-start(bf16[32,2048]{1,0:T(8,128)(2,1)S(1)} %get-tuple-element.64), channel_id=1, source_target_pairs={{0,16},{4,20},{8,24},{12,28},{16,0},{20,4},{24,8},{28,12},{1,17},{... | collective-permute-start | bytes 393224 | tf_op jit(solution)/shard_map/ppermute | solution.py:500
  116.6 6.2 %collective-permute-start.28 = (bf16[32,2048]{1,0:T(8,128)(2,1)S(1)}, bf16[32,2048]{1,0:T(8,128)(2,1)S(1)}, u32[]{:S(2)}, u32[]{:S(2)}) collective-permute-start(bf16[32,2048]{1,0:T(8,128)(2,1)S(1)} %get-tuple-element.65), channel_id=1, source_target_pairs={{0,24},{4,28},{8,16},{12,20},{16,8},{20,12},{24,0},{28,4},{1,25},{... | collective-permute-start | bytes 393224 | tf_op jit(solution)/shard_map/ppermute | solution.py:500
  116.7 32.1 %collective-permute-start.22 = (bf16[32,2048]{1,0:T(8,128)(2,1)S(1)}, bf16[32,2048]{1,0:T(8,128)(2,1)S(1)}, u32[]{:S(2)}, u32[]{:S(2)}) collective-permute-start(bf16[32,2048]{1,0:T(8,128)(2,1)S(1)} %finish.1.refs_0_), channel_id=1, source_target_pairs={{0,1},{1,0},{2,3},{3,2},{4,5},{5,4},{6,7},{7,6},{8,9},{9,8},{10,11... | collective-permute-start | bytes 393224 | tf_op jit(solution)/shard_map/ppermute | solution.py:500
  120.1 28.6 %collective-permute-start.24 = (bf16[32,2048]{1,0:T(8,128)(2,1)S(1)}, bf16[32,2048]{1,0:T(8,128)(2,1)S(1)}, u32[]{:S(2)}, u32[]{:S(2)}) collective-permute-start(bf16[32,2048]{1,0:T(8,128)(2,1)S(1)} %collective-permute-done.23.refs_2_), channel_id=1, source_target_pairs={{0,1},{1,0},{2,3},{3,2},{4,5},{5,4},{6,7},{7,6},{8,9},{9,8},{10,11... | collective-permute-start | bytes 393224 | tf_op jit(solution)/shard_map/ppermute | solution.py:500
  125.8 5.7 %collective-permute-start.31 = (bf16[8,2048]{1,0:T(8,128)(2,1)S(1)}, bf16[8,2048]{1,0:T(8,128)(2,1)S(1)}, u32[]{:S(2)}, u32[]{:S(2)}) collective-permute-start(bf16[8,2048]{1,0:T(8,128)(2,1)S(1)} %get-tuple-element.69), channel_id=1, source_target_pairs={{0,3},{1,2},{2,1},{3,0},{4,7},{5,6},{6,5},{7,4},{8,11},{9,10},{10,... | collective-permute-start | bytes 98312 | tf_op jit(solution)/shard_map/ppermute | solution.py:500
  131.9 7.1 %collective-permute-start.34 = (bf16[8,2048]{1,0:T(8,128)(2,1)S(1)}, bf16[8,2048]{1,0:T(8,128)(2,1)S(1)}, u32[]{:S(2)}, u32[]{:S(2)}) collective-permute-start(bf16[8,2048]{1,0:T(8,128)(2,1)S(1)} %norm_grad.1.refs_4_), channel_id=1, source_target_pairs={{0,3},{1,2},{2,1},{3,0},{4,7},{5,6},{6,5},{7,4},{8,11},{9,10},{10,... | collective-permute-start | bytes 98312 | tf_op jit(solution)/shard_map/ppermute | solution.py:500
  133.7 5.3 %collective-permute-start.33 = (bf16[8,2048]{1,0:T(8,128)(2,1)S(1)}, bf16[8,2048]{1,0:T(8,128)(2,1)S(1)}, u32[]{:S(2)}, u32[]{:S(2)}) collective-permute-start(bf16[8,2048]{1,0:T(8,128)(2,1)S(1)} %norm_grad.1.refs_4_), channel_id=1, source_target_pairs={{0,2},{1,3},{2,0},{3,1},{4,6},{5,7},{6,4},{7,5},{8,10},{9,11},{10,... | collective-permute-start | bytes 98312 | tf_op jit(solution)/shard_map/ppermute | solution.py:500
  133.7 5.3 %collective-permute-start.32 = (bf16[8,2048]{1,0:T(8,128)(2,1)S(1)}, bf16[8,2048]{1,0:T(8,128)(2,1)S(1)}, u32[]{:S(2)}, u32[]{:S(2)}) collective-permute-start(bf16[8,2048]{1,0:T(8,128)(2,1)S(1)} %norm_grad.1.refs_4_), channel_id=1, source_target_pairs={{0,1},{1,0},{2,3},{3,2},{4,5},{5,4},{6,7},{7,6},{8,9},{9,8},{10,11... | collective-permute-start | bytes 98312 | tf_op jit(solution)/shard_map/ppermute | solution.py:500
  140.6 5.6 %collective-permute-start.37 = (f32[32,128]{1,0:T(8,128)S(1)}, f32[32,128]{1,0:T(8,128)S(1)}, u32[]{:S(2)}, u32[]{:S(2)}) collective-permute-start(f32[32,128]{1,0:T(8,128)S(1)} %get-tuple-element.71.refs_0_), channel_id=1, source_target_pairs={{0,3},{1,2},{2,1},{3,0},{4,7},{5,6},{6,5},{7,4},{8,11},{9,10},{10,... | collective-permute-start | bytes 49160 | tf_op jit(solution)/shard_map/ppermute | solution.py:500
  (41 other events, 109.7 us)
where the time goes:
time: 151 us; the launch traced here: 150 us
  starting transfers between devices  47.8 us (32%)
  waiting for transfers between devices  43.5 us (29%)
  local copies, waits for them, and re-layouts  36 us (24%)
  Pallas kernels  21.3 us (14%)
    ppermute x38, waiting for transfers between devices, swap(): return lax.ppermute(value, axis, [(i, i ^ step) for i in range(count)])  43.5 us
    ppermute x38, starting transfers between devices, swap(): return lax.ppermute(value, axis, [(i, i ^ step) for i in range(count)])  40.5 us
    unnamed x66, local copies, waits for them, and re-layouts  36 us
    pallas_call x18, Pallas kernels, run(): pl.pallas_call(kernel, out_shape=outs, in_specs=specs, out_specs=jax.tree...  18.9 us
    all_to_all x2, starting transfers between devices, send_all(): return lax.all_to_all(value, axis, split_axis=0, concat_axis=0, tiled=True)  7.23 us
  transfers between devices with their start and end apart: 40, of which 18 were waited for; matrix products, arithmetic and copies ran while one was open for 0% of the time, Pallas kernels for 7%

commit v1 on v0

--- a/solution.py
+++ b/solution.py
@@ -9,9 +9,11 @@
 
 CAPX = 10
 SLOTS = 16
-SEND = 32
+SEND = 24
 EPS = 1e-06
-VMEM_BYTES = 24 * 1024 * 1024
+VMEM_BYTES = 16 * 1024 * 1024
+PACK_BYTES = 60 * 1024 * 1024
+ATTEND_BYTES = 58 * 1024 * 1024
 F32 = jnp.float32
 BF16 = jnp.bfloat16
 
@@ -77,64 +79,13 @@
     out_ref[...] = jnp.concatenate([part.astype(F32) for part in parts], axis=0).astype(BF16)
 
 
-def hold_kernel(*refs):
-    count = (len(refs) - 1) // 2
-    copies = []
-    sems = refs[-1]
-    for i in range(count):
-        far_ref, near_ref = refs[i], refs[count + i]
-        chunk = far_ref.shape[0] // sems.shape[1]
-        for j in range(sems.shape[1]):
-            mine = pl.ds(j * chunk, chunk)
-            copies.append(pltpu.make_async_copy(far_ref.at[mine], near_ref.at[mine], sems.at[i, j]))
-            copies[-1].start()
-    for copy in copies:
-        copy.wait()
-
-
-def plan_kernel(*refs, blocks, groups, merged_rows, row_share):
-    near_refs = refs[:blocks]
-    routes_ref, gates_ref, text_ref, gain_ref, cot_ref, _ = refs[blocks : blocks + 6]
-    slots_ref, placed_ref, comb_ref, send_ref = refs[blocks + 6 :]
-    tokens = text_ref.shape[0]
-    share = merged_rows // row_share
-    rows = blocks * merged_rows
+def route_kernel(routes_ref, gates_ref, comb_ref, pick_ref, factor_ref, *, groups, share):
+    blocks = comb_ref.shape[1] // SLOTS
+    tokens = routes_ref.shape[1]
     me, expert_index = lax.axis_index("blk"), lax.axis_index("expert")
     member = expert_index // groups
-    meta = [ref[...].astype(F32) for ref in near_refs]
-    mine = (2 * me + member).astype(F32)
-    hits = [jnp.sum((part[:8] == mine).astype(F32), axis=0, keepdims=True) for part in meta]
-    hit = jnp.concatenate(hits, axis=0)
-    dest = jnp.concatenate([part[9:10] for part in meta], axis=0)
     before = (iota((tokens, tokens), 0) < iota((tokens, tokens), 1)).astype(BF16)
-    rank = dot(hit, before)
-
-    def row_of(col):
-        inner = col % merged_rows
-        return ((inner // row_share) ^ expert_index) * row_share + inner % row_share
-
-    def place_of(col):
-        return ((col // merged_rows) ^ me) * merged_rows + row_of(col)
-
-    spread = (iota((128, rows), 0) == row_of(iota((128, rows), 1))).astype(F32)
-    own_block = iota((blocks, rows), 1) // merged_rows == iota((blocks, rows), 0)
-    dest_row = jnp.sum(jnp.where(own_block, dot(dest, spread), 0.0), axis=0, keepdims=True)
-    dest_row = dest_row.astype(jnp.int32) ^ me
-    dest_hit = (iota((blocks, rows), 0) == dest_row).astype(F32)
-    rows_before = place_of(iota((rows, rows), 0)) < place_of(iota((rows, rows), 1))
-    earlier = dot(dest_hit, rows_before.astype(F32))
-    slot = jnp.sum(dest_hit * earlier, axis=0, keepdims=True).astype(jnp.int32)
-    at_token = (iota((tokens, rows), 0) == slot).astype(F32)
-    row_hit = jnp.sum(dest_hit * dot(hit, at_token), axis=0, keepdims=True)
-    row_rank = jnp.sum(dest_hit * dot(rank, at_token), axis=0, keepdims=True).astype(jnp.int32)
-    slot_id = (dest_row ^ me) * SLOTS + row_rank
-    slot_count = slots_ref.shape[0]
-    chosen = (iota((slot_count, rows), 0) == slot_id) & (row_hit > 0.5)
-    slots_ref[...] = chosen.astype(F32).astype(BF16)
-    placed = jnp.where(dest_row == 0, at_token, 0.0).astype(BF16)
-    placed_ref[...] = placed
-
-    pair_of = 2 * iota((blocks, tokens), 0) + member
+    pair_of = 2 * (iota((blocks, tokens), 0) ^ me) + member
     out_hit = jnp.zeros((blocks, tokens), F32)
     out_gate = jnp.zeros((blocks, tokens), F32)
     for k in range(routes_ref.shape[0]):
@@ -167,20 +118,68 @@
     place = iota(hits.shape, 0) % SEND
     input_pick = jnp.where((place < CAPX) & (ranks == place), hits, 0.0)
     back_pick = jnp.where((place >= CAPX) & (place < 2 * CAPX) & (ranks == place - CAPX), hits, 0.0)
-    back_gate = jnp.sum(back_pick * gates, axis=1, keepdims=True)
-    send_rows = blocks * SEND
-    source = iota((send_rows, rows), 0)
-    kept = source % SEND - 2 * CAPX
-    wanted = ((source // SEND) ^ me) * merged_rows + kept
-    row_pick = (kept >= 0) & (kept < row_share) & (iota((send_rows, rows), 1) == wanted)
-    cot_pick = dot_nt(row_pick.astype(F32).astype(BF16), placed)
-    cot_row = iota((send_rows, 1), 0) % SEND >= 2 * CAPX
-    factor = jnp.where(cot_row, 1.0, back_gate)
+    pick_ref[0] = input_pick.astype(BF16)
+    pick_ref[1] = back_pick.astype(BF16)
+    factor = jnp.sum(back_pick * gates, axis=1, keepdims=True)
+    factor_ref[...] = jnp.broadcast_to(factor, factor_ref.shape)
+
+
+def dispatch_kernel(pick_ref, factor_ref, text_ref, gain_ref, cot_ref, *send_refs):
     text = text_ref[...].astype(F32)
     scale = lax.rsqrt(jnp.mean(text * text, axis=1, keepdims=True) + EPS)
     h_rows = (text * scale * gain_ref[...]).astype(BF16)
-    send = dot(input_pick, h_rows) + factor * dot(back_pick + cot_pick, cot_ref[...])
-    send_ref[...] = send.astype(BF16)
+    factor = factor_ref[:, :1]
+    send = dot(pick_ref[0], h_rows) + factor * dot(pick_ref[1], cot_ref[...])
+    send = send.astype(BF16)
+    count = 2 * SEND
+    for k, ref in enumerate(send_refs):
+        ref[...] = send[k * count : (k + 1) * count]
+
+
+def plan_kernel(
+    meta_ref, cot_ref, slots_ref, placed_ref, back_ref, *, blocks, groups, merged_rows, row_share
+):
+    tokens = cot_ref.shape[0]
+    rows = blocks * merged_rows
+    me, expert_index = lax.axis_index("blk"), lax.axis_index("expert")
+    member = expert_index // groups
+    meta = [meta_ref[k * 16 : (k + 1) * 16].astype(F32) for k in range(blocks)]
+    mine = (2 * me + member).astype(F32)
+    hits = [jnp.sum((part[:8] == mine).astype(F32), axis=0, keepdims=True) for part in meta]
+    hit = jnp.concatenate(hits, axis=0)
+    dest = jnp.concatenate([part[9:10] for part in meta], axis=0)
+    before = (iota((tokens, tokens), 0) < iota((tokens, tokens), 1)).astype(BF16)
+    rank = dot(hit, before)
+
+    def row_of(col):
+        inner = col % merged_rows
+        return ((inner // row_share) ^ expert_index) * row_share + inner % row_share
+
+    def place_of(col):
+        return ((col // merged_rows) ^ me) * merged_rows + row_of(col)
+
+    spread = (iota((128, rows), 0) == row_of(iota((128, rows), 1))).astype(F32)
+    own_block = iota((blocks, rows), 1) // merged_rows == iota((blocks, rows), 0)
+    dest_row = jnp.sum(jnp.where(own_block, dot(dest, spread), 0.0), axis=0, keepdims=True)
+    dest_row = dest_row.astype(jnp.int32) ^ me
+    dest_hit = (iota((blocks, rows), 0) == dest_row).astype(F32)
+    rows_before = place_of(iota((rows, rows), 0)) < place_of(iota((rows, rows), 1))
+    earlier = dot(dest_hit, rows_before.astype(F32))
+    slot = jnp.sum(dest_hit * earlier, axis=0, keepdims=True).astype(jnp.int32)
+    at_token = (iota((tokens, rows), 0) == slot).astype(F32)
+    row_hit = jnp.sum(dest_hit * dot(hit, at_token), axis=0, keepdims=True)
+    row_rank = jnp.sum(dest_hit * dot(rank, at_token), axis=0, keepdims=True).astype(jnp.int32)
+    slot_id = dest_row * SLOTS + row_rank
+    slot_count = slots_ref.shape[0]
+    chosen = (iota((slot_count, rows), 0) == slot_id) & (row_hit > 0.5)
+    slots_ref[...] = chosen.astype(F32).astype(BF16)
+    placed = jnp.where(dest_row == 0, at_token, 0.0).astype(BF16)
+    placed_ref[...] = placed
+    back_rows = blocks * row_share
+    source = iota((back_rows, rows), 0)
+    wanted = source // row_share * merged_rows + source % row_share
+    row_pick = (iota((back_rows, rows), 1) == wanted).astype(F32).astype(BF16)
+    back_ref[...] = dot(dot_nt(row_pick, placed), cot_ref[...]).astype(BF16)
 
 
 def flat_gain(gain_ref):
@@ -190,12 +189,22 @@
 def attend_kernel(*refs, blocks, share, row_share):
     query_ref, gain_ref, weight_ref = refs[:3]
     near_refs = refs[3 : 3 + blocks]
-    merged_ref, *message_refs = refs[3 + blocks :]
+    merged_ref, meta_ref, *message_refs = refs[3 + blocks : 5 + blocks + share]
+    near_weight_ref, sems = refs[5 + blocks + share :]
+    chunk = weight_ref.shape[0] // sems.shape[0]
+    copies = []
+    for i in range(sems.shape[0]):
+        mine = pl.ds(i * chunk, chunk)
+        copies.append(
+            pltpu.make_async_copy(weight_ref.at[mine], near_weight_ref.at[mine], sems.at[i])
+        )
+        copies[-1].start()
     heads, size, patches = query_ref.shape
     rows, features = merged_ref.shape
     width = weight_ref.shape[1]
     depth = heads * size
     near = [ref[...].astype(F32) for ref in near_refs]
+    meta_ref[...] = jnp.concatenate([part[2 * depth :] for part in near], axis=0).astype(BF16)
     key_ids = jnp.concatenate([part[2 * depth + 8 : 2 * depth + 9] for part in near], axis=1)
     eye = iota((patches, patches), 0) == iota((patches, patches), 1)
     own_ids = jnp.sum(jnp.where(eye, key_ids[:, :patches], 0.0), axis=1, keepdims=True)
@@ -229,7 +238,9 @@
     extra = iota((8, features), 0)
     gain_rows = jnp.where(extra == 0, gain_high, jnp.where(extra == 1, gain - gain_high, 0.0))
     left = jnp.concatenate([centered * gain, gain_rows], axis=0)
-    product = dot(left, weight_ref[...])
+    for copy in copies:
+        copy.wait()
+    product = dot(left, near_weight_ref[...])
     gain_sum = product[rows : rows + 1] + product[rows + 1 : rows + 2]
     piece = width // row_share
     pieces = [gain_sum[:, j * piece : (j + 1) * piece] for j in range(row_share)]
@@ -262,13 +273,29 @@
     out_ref[:, width:] = put_scalars([mean, inv_std], row_share).astype(BF16)
 
 
-def stack_kernel(*refs):
+def stack_kernel(_, *refs):
     *part_refs, out_ref = refs
     out_ref[...] = stacked(part_refs)
 
 
 def stacked(part_refs):
     return jnp.concatenate([ref[...].astype(F32) for ref in part_refs], axis=0).astype(BF16)
+
+
+def by_chip(own_refs, sibling_ref):
+    parts = []
+    sibling = sibling_ref[...].astype(F32)
+    for k, own_ref in enumerate(own_refs):
+        half = own_ref.shape[0] // 2
+        parts.append(own_ref[...].astype(F32)[:half])
+        parts.append(sibling[k * half : (k + 1) * half])
+    return jnp.concatenate(parts, axis=0).astype(BF16)
+
+
+def other_half_kernel(*refs, count):
+    out_ref = refs[-1]
+    parts = [ref[...].astype(F32)[ref.shape[0] // 2 :] for ref in refs[:count]]
+    out_ref[...] = jnp.concatenate(parts, axis=0).astype(BF16)
 
 
 def slot_pick(slot_count, send_rows, shift):
@@ -278,57 +305,67 @@
     return pick.astype(F32)
 
 
+def early_kernel(down_ref, *refs):
+    *early_refs, sibling_ref, text_out, grad_out = refs
+    slot_count = text_out.shape[0]
+    early = by_chip(early_refs, sibling_ref)
+    text_out[...] = dot(slot_pick(slot_count, early.shape[0], 0), early).astype(BF16)
+    back_rows = dot(slot_pick(slot_count, early.shape[0], CAPX), early).astype(BF16)
+    grad_out[...] = dot_nt(back_rows, down_ref[0])
+
+
 def forward_kernel(*refs, blocks):
-    slots_ref, gain_ref, gate_ref, up_ref, down_ref, early_ref = refs[:6]
+    slots_ref, gain_ref, gate_ref, up_ref, down_ref, text_ref = refs[:6]
     vision_refs = refs[6 : 6 + blocks]
-    gate_out, up_out, down_out, h_ref, sum_ref = refs[6 + blocks :]
-    hidden, width = gate_ref.shape
-    slot_count = slots_ref.shape[0]
+    gate_out, up_out, *down_refs = refs[6 + blocks : -2]
+    h_ref, sum_ref = refs[-2:]
+    _, hidden, width = gate_ref.shape
     chosen = slots_ref[...]
     is_vision = jnp.sum(chosen.astype(F32), axis=1, keepdims=True) > 0.5
     vision = jnp.concatenate([ref[:, :width] for ref in vision_refs], axis=0)
     inputs = dot(chosen, vision)
     scale = lax.rsqrt(jnp.mean(inputs * inputs, axis=1, keepdims=True) + EPS)
     normed = inputs * scale * gain_ref[...]
-    early = early_ref[...]
-    text_rows = dot(slot_pick(slot_count, early.shape[0], 0), early)
-    h_ref[...] = jnp.where(is_vision, normed, text_rows).astype(BF16)
+    h_ref[...] = jnp.where(is_vision, normed, text_ref[...].astype(F32)).astype(BF16)
     tile = tile_of(hidden)
     for i in range(hidden // tile):
         mine = slice(i * tile, (i + 1) * tile)
-        gate_pre = dot_nt(h_ref[...], gate_ref[mine])
-        up_proj = dot_nt(h_ref[...], up_ref[mine])
+        gate_pre = dot_nt(h_ref[...], gate_ref[0, mine])
+        up_proj = dot_nt(h_ref[...], up_ref[0, mine])
         gate_out[:, mine] = gate_pre
         up_out[:, mine] = up_proj
         activated = gate_pre * jax.nn.sigmoid(gate_pre) * up_proj
-        product = dot(activated, down_ref[mine])
+        product = dot(activated, down_ref[0, mine])
         sum_ref[...] = product if i == 0 else sum_ref[...] + product
-    down_out[...] = sum_ref[...].astype(BF16)
+    count = 2 * SLOTS
+    for k, ref in enumerate(down_refs):
+        ref[...] = sum_ref[k * count : (k + 1) * count].astype(BF16)
 
 
 def backward_kernel(
-    slots_ref, early_ref, gate_in, up_in, gate_ref, up_ref, down_ref, even_ref, odd_ref,
-    back_ref, sum_ref, *, blocks,
+    slots_ref, grad_ref, gate_in, up_in, cot_ref, gate_ref, up_ref, even_ref, odd_ref, sum_ref,
+    *, blocks,
 ):
-    hidden = gate_ref.shape[0]
-    slot_count = slots_ref.shape[0]
-    early = early_ref[...]
-    back_ref[...] = dot(slot_pick(slot_count, early.shape[0], CAPX), early).astype(BF16)
+    hidden = gate_ref.shape[1]
     tile = tile_of(hidden)
     for i in range(hidden // tile):
         mine = slice(i * tile, (i + 1) * tile)
-        act_grad = dot_nt(back_ref[...], down_ref[mine])
+        act_grad = grad_ref[:, mine]
         gate_pre, up_proj = gate_in[:, mine], up_in[:, mine]
         sigmoid = jax.nn.sigmoid(gate_pre)
         gate_grad = act_grad * up_proj * sigmoid * (1.0 + gate_pre * (1.0 - sigmoid))
         up_grad = act_grad * gate_pre * sigmoid
-        product = dot(gate_grad, gate_ref[mine]) + dot(up_grad, up_ref[mine])
+        product = dot(gate_grad, gate_ref[0, mine]) + dot(up_grad, up_ref[0, mine])
         sum_ref[...] = product if i == 0 else sum_ref[...] + product
-    grads = dot_tn(slots_ref[...], sum_ref[...].astype(BF16)).astype(BF16)
-    rows = grads.shape[0] // blocks
+    grads = dot_tn(slots_ref[...], sum_ref[...].astype(BF16))
+    cots = cot_ref[...].astype(F32)
+    rows, row_share = grads.shape[0] // blocks, cots.shape[0] // blocks
+    parts = ([], [])
     for k in range(blocks):
-        to_ref = odd_ref if k % 2 else even_ref
-        to_ref[k // 2 * rows : (k // 2 + 1) * rows] = grads[k * rows : (k + 1) * rows]
+        parts[k % 2].append(grads[k * rows : (k + 1) * rows])
+        parts[k % 2].append(cots[k * row_share : (k + 1) * row_share])
+    even_ref[...] = jnp.concatenate(parts[0], axis=0).astype(BF16)
+    odd_ref[...] = jnp.concatenate(parts[1], axis=0).astype(BF16)
 
 
 def tile_of(hidden):
@@ -346,9 +383,9 @@
 
 def pair_sum_kernel(own_ref, sibling_ref, *out_refs):
     rows = out_refs[0].shape[0]
+    total = own_ref[...].astype(F32) + sibling_ref[...].astype(F32)
     for k, out_ref in enumerate(out_refs):
-        mine = slice(k * rows, (k + 1) * rows)
-        out_ref[...] = (own_ref[mine].astype(F32) + sibling_ref[mine].astype(F32)).astype(BF16)
+        out_ref[...] = total[k * rows : (k + 1) * rows].astype(BF16)
 
 
 def total_of(part_refs):
@@ -359,22 +396,24 @@
 
 
 def chip_sum_kernel(*refs, count):
-    out_refs = refs[count:]
+    cot_ref, *out_refs = refs[count:]
     total = total_of(refs[:count])
-    rows = out_refs[0].shape[0]
+    rows = cot_ref.shape[0]
     for k, out_ref in enumerate(out_refs):
         out_ref[...] = total[k * rows : (k + 1) * rows].astype(BF16)
-
-
-def combine_kernel(comb_ref, rows_ref, keep_ref, send_ref):
-    rows = rows_ref[...]
+    cot_ref[...] = total[len(out_refs) * rows :].astype(BF16)
+
+
+def combine_kernel(comb_ref, *refs):
+    *part_refs, sibling_ref, keep_ref, send_ref = refs
+    rows = by_chip(part_refs, sibling_ref)
     total = dot_tn(comb_ref[0], rows) + dot_tn(comb_ref[1], rows)
     half = keep_ref.shape[0]
     keep_ref[...] = total[:half]
     send_ref[...] = total[half:].astype(BF16)
 
 
-def halve_kernel(own_ref, arrived_ref, keep_ref, send_ref):
+def halve_kernel(own_ref, arrived_ref, _, keep_ref, send_ref):
     total = own_ref[...] + arrived_ref[...].astype(F32)
     half = keep_ref.shape[0]
     keep_ref[...] = total[:half]
@@ -382,7 +421,7 @@
 
 
 def finish_kernel(placed_ref, text_ref, own_ref, arrived_ref, *refs):
-    *vision_refs, out_ref = refs
+    *vision_refs, _, out_ref = refs
     count, width = out_ref.shape
     tokens = placed_ref.shape[0]
     first = lax.axis_index("expert") * count
@@ -403,14 +442,11 @@
         out_ref[pl.ds(first, count), :] = ref[...]
 
 
-def norm_grad_kernel(own_ref, gain_ref, early_ref, *refs):
+def norm_grad_kernel(own_ref, gain_ref, cot_ref, *refs):
     *part_refs, out_ref = refs
-    row_share, width = out_ref.shape
+    width = out_ref.shape[1]
     hidden = total_of(part_refs)
-    early = early_ref[...]
-    send_rows = early.shape[0]
-    pick = iota((row_share, send_rows), 1) % SEND == iota((row_share, send_rows), 0) + 2 * CAPX
-    cotangent = dot(pick.astype(F32), early)
+    cotangent = cot_ref[...].astype(F32)
     inputs = own_ref[:, :width].astype(F32)
     scale = lax.rsqrt(jnp.mean(inputs * inputs, axis=1, keepdims=True) + EPS)
     pulled = hidden * gain_ref[...]
@@ -471,24 +507,48 @@
     return pl.BlockSpec(memory_space=memory_space)
 
 
-def run(kernel, outs, *args, far=(), scratch=(), cost=1.0, name=None):
+def run(kernel, outs, *args, far=(), scratch=(), cost=1.0, vmem=VMEM_BYTES, name=None):
     specs = [whole()] * len(args)
     for place in far:
-        specs[place] = whole(pltpu.HBM)
+        specs[place] = whole(pl.ANY)
     return pl.pallas_call(
         kernel,
         out_shape=outs,
         in_specs=specs,
         out_specs=jax.tree.map(lambda _: whole(), outs),
         scratch_shapes=scratch,
-        compiler_params=pltpu.CompilerParams(vmem_limit_bytes=VMEM_BYTES),
+        compiler_params=pltpu.CompilerParams(vmem_limit_bytes=vmem),
         cost_estimate=microseconds(cost),
         name=name,
     )(*args)
 
 
+def to_sibling(parts, deps, name):
+    rows, width = parts[0].shape
+    half = run(
+        functools.partial(other_half_kernel, count=len(parts)),
+        shape((len(parts) * rows // 2, width)), *parts, *deps,
+        far=range(len(parts), len(parts) + len(deps)), cost=0.3, name=name,
+    )
+    return swap(half, "blk", 1)
+
+
 def microseconds(time):
     return pl.CostEstimate(flops=0, transcendentals=0, bytes_accessed=int(time * 3e6))
+
+
+def after(values, deps):
+    count = len(values)
+    return pl.pallas_call(
+        lambda *refs: None,
+        out_shape=[shape(value.shape, value.dtype) for value in values],
+        in_specs=[whole(pl.ANY)] * (count + len(deps)),
+        out_specs=[whole(pl.ANY)] * count,
+        input_output_aliases={i: i for i in range(count)},
+        compiler_params=pltpu.CompilerParams(vmem_limit_bytes=VMEM_BYTES),
+        cost_estimate=microseconds(0.1),
+        name="after",
+    )(*values, *deps)
 
 
 def shape(dims, dtype=BF16):
@@ -508,29 +568,16 @@
     return trade([value] * lax.axis_size(axis), axis)
 
 
-def gather_blocks(value):
-    near = {0: value}
-    for k in range(2, lax.axis_size("blk"), 2):
-        near[k] = swap(value, "blk", k)
-    for k in list(near):
-        near[k + 1] = swap(near[k], "blk", 1)
-    return [near[k] for k in sorted(near)]
-
-
-def hold(arrays, after=None, name=None):
-    if after is not None:
-        *arrays, _ = lax.optimization_barrier((*arrays, after))
-    chunks = 3 if arrays[0].shape[0] % 48 == 0 else 1
-    return run(
-        hold_kernel, [shape(array.shape) for array in arrays], *arrays,
-        far=tuple(range(len(arrays))),
-        scratch=[pltpu.SemaphoreType.DMA((len(arrays), chunks))],
-        cost=sum(array.size for array in arrays) / 1e6, name=name,
-    )
-
-
-def send_all(value, axis):
-    return lax.all_to_all(value, axis, split_axis=0, concat_axis=0, tiled=True)
+def gather_blocks(value, deps=None):
+    own = [value] + [swap(value, "blk", k) for k in range(2, lax.axis_size("blk"), 2)]
+    if deps is not None:
+        own = own[:1] + list(after(own[1:], deps))
+    sibling = [swap(part, "blk", 1) for part in own]
+    return [part for pair in zip(own, sibling) for part in pair]
+
+
+def to_chips(parts):
+    return [parts[0]] + [swap(parts[k], "blk", 2 * k) for k in range(1, len(parts))]
 
 
 def body(
@@ -560,115 +607,119 @@
         pack_kernel, shape((2 * depth + 16, patches)), *small, far=range(5),
         scratch=[pltpu.VMEM(array.shape, array.dtype) for array in small]
         + [pltpu.SemaphoreType.DMA((5,))],
-        name="pack",
-    )
-    near = gather_blocks(local)
+        vmem=PACK_BYTES, name="pack",
+    )
+    comb, pick, factor = run(
+        functools.partial(route_kernel, groups=groups, share=share),
+        [
+            shape((2, slot_count, tokens)), shape((2, blocks * SEND, tokens)),
+            shape((blocks * SEND, 128), F32),
+        ],
+        routes_t, gates_t, cost=3.0, name="route",
+    )
+    send = run(
+        dispatch_kernel, [shape((2 * SEND, width))] * (blocks // 2),
+        pick, factor, text, gain_row, cotangent, cost=2.0, name="dispatch",
+    )
+    near = gather_blocks(local, send)
+    early = to_chips(after(send, near[1:]))
+
     weight_flat = merge_weight.reshape(features, width)
-    (weight_near,) = hold([weight_flat], name="hold_merge")
-
     message_width = width + width // row_share + 128
-    merged, *message = run(
+    merged, meta, *message = run(
         functools.partial(attend_kernel, blocks=blocks, share=share, row_share=row_share),
-        [shape((rows, features))] + [shape((row_share, message_width))] * share,
-        queries, merge_gain, weight_near, *near, cost=4.0, name="attend",
-    )
-
-    def fixed(*dims):
-        return pl.BlockSpec(dims, lambda i: (0,) * len(dims))
-
-    meta_spec = pl.BlockSpec((16, patches), lambda i: (2 * depth // 16, 0))
-    plan_outs = [
-        shape((slot_count, all_rows)), shape((tokens, all_rows)), shape((2, slot_count, tokens)),
-        shape((blocks * SEND, width)),
-    ]
-    slots, placed, comb, send = pl.pallas_call(
+        [shape((rows, features)), shape((blocks * 16, patches))] + [shape((row_share, message_width))] * share,
+        queries, merge_gain, weight_flat, *near, far=(2,), cost=4.0, vmem=ATTEND_BYTES,
+        scratch=[
+            pltpu.VMEM((features, width), BF16),
+            pltpu.SemaphoreType.DMA((4 if features % 64 == 0 else 1,)),
+        ],
+        name="attend",
+    )
+
+    slots, placed, back_cots = run(
         functools.partial(
             plan_kernel, blocks=blocks, groups=groups, merged_rows=rows, row_share=row_share
         ),
-        grid=(1,),
-        in_specs=[meta_spec] * blocks
-        + [
-            fixed(*routes_t.shape), fixed(*gates_t.shape), fixed(tokens, width), fixed(1, width),
-            fixed(tokens, width), whole(pl.ANY),
+        [
+            shape((slot_count, all_rows)), shape((tokens, all_rows)),
+            shape((blocks * row_share, width)),
         ],
-        out_specs=[fixed(*out.shape) for out in plan_outs],
-        out_shape=plan_outs,
-        compiler_params=pltpu.CompilerParams(vmem_limit_bytes=VMEM_BYTES),
-        cost_estimate=microseconds(2.0),
-        name="plan",
-    )(*near, routes_t, gates_t, text, gain_row, cotangent, merged)
-    early = send_all(send.reshape(blocks, SEND, width), "blk").reshape(blocks * SEND, width)
-
+        meta, cotangent, cost=1.5, name="plan",
+    )
     message = trade(message, "expert")
+    text_rows, act_grad = run(
+        early_kernel, [shape((slot_count, width)), shape((slot_count, hidden), F32)],
+        w_down, *early, to_sibling(early, message[1:], "early_half"), cost=3.0, name="early",
+    )
     own = run(
         functools.partial(merge_kernel, width=width, features=features),
         shape((row_share, width + 128)), *message, cost=0.2, name="merge",
     )
     block_rows = run(
-        stack_kernel, shape((rows, width + 128)), *spread_out(own, "expert"), cost=0.2, name="stack"
+        stack_kernel, shape((rows, width + 128)), text_rows, *spread_out(own, "expert"),
+        far=(0,), cost=0.2, name="stack",
     )
     vision = gather_blocks(block_rows)
-    gate_near, up_near, down_near = hold(
-        [w_gate[0], w_up[0], w_down[0]], after=own, name="hold_experts"
-    )
-
-    gate_pre, up_proj, down = run(
+
+    gate_pre, up_proj, *down = run(
         functools.partial(forward_kernel, blocks=blocks),
         [
             shape((slot_count, hidden), F32), shape((slot_count, hidden), F32),
-            shape((slot_count, width)),
-        ],
-        slots, gain_row, gate_near, up_near, down_near, early, *vision,
+        ] + [shape((2 * SLOTS, width))] * (blocks // 2),
+        slots, gain_row, w_gate, w_up, w_down, text_rows, *vision,
         scratch=[pltpu.VMEM((slot_count, width), BF16), pltpu.VMEM((slot_count, width), F32)],
-        cost=5.0, name="forward",
-    )
-    returned = send_all(down.reshape(blocks, SLOTS, width), "blk").reshape(slot_count, width)
+        cost=4.0, name="forward",
+    )
+    block = rows + row_share
     even, odd = run(
         functools.partial(backward_kernel, blocks=blocks),
-        [shape((all_rows // 2, width))] * 2,
-        slots, early, gate_pre, up_proj, gate_near, up_near, down_near,
-        scratch=[pltpu.VMEM((slot_count, width), BF16), pltpu.VMEM((slot_count, width), F32)],
-        cost=5.0, name="backward",
+        [shape((blocks // 2 * block, width))] * 2,
+        slots, act_grad, gate_pre, up_proj, back_cots, w_gate, w_up,
+        scratch=[pltpu.VMEM((slot_count, width), F32)],
+        cost=4.0, name="backward",
     )
     grads = run(
-        pair_sum_kernel, [shape((rows, width))] * (blocks // 2), even, swap(odd, "blk", 1),
+        pair_sum_kernel, [shape((block, width))] * (blocks // 2), even, swap(odd, "blk", 1),
         cost=0.2, name="pair_sum",
     )
-    grads = [grads[0]] + [swap(grads[k], "blk", 2 * k) for k in range(1, blocks // 2)]
-    grads = run(
+    grads = to_chips(grads)
+    returned = to_chips(after(down, grads[1:2]))
+    cot_rows, *grads = run(
         functools.partial(chip_sum_kernel, count=blocks // 2),
-        [shape((row_share, width))] * share, *grads, cost=0.2, name="chip_sum",
+        [shape((row_share, width))] * (share + 1), *grads, cost=0.2, name="chip_sum",
     )
     grads = trade(grads, "expert")
     vision_grad = run(
-        norm_grad_kernel, shape((row_share, width)), own, gain_row, early, *grads,
+        norm_grad_kernel, shape((row_share, width)), own, gain_row, cot_rows, *grads,
         cost=0.3, name="norm_grad",
     )
-    (weight_again,) = hold([weight_flat], after=down, name="hold_merge_again")
     normed_grad, sums = run(
         merge_grad_kernel,
         [shape((rows, features), F32), shape((rows, 128), F32)],
-        merge_gain, merged, block_rows, weight_again, *spread_out(vision_grad, "expert"),
+        merge_gain, merged, block_rows, weight_flat, *spread_out(vision_grad, "expert"),
         cost=2.5, name="merge_grad",
     )
+    sums_own = sums
     sums = spread_out(sums, "expert")
 
     count = tokens // 2
     kept, sent = run(
-        combine_kernel, [shape((count, width), F32), shape((count, width))], comb, returned,
-        cost=0.5, name="combine",
+        combine_kernel, [shape((count, width), F32), shape((count, width))], comb, *returned,
+        to_sibling(returned, grads[:1], "returned_half"), cost=0.5, name="combine",
     )
     step = 1
     while count > part:
         count //= 2
         kept, sent = run(
             halve_kernel, [shape((count, width), F32), shape((count, width))],
-            kept, swap(sent, "expert", step), cost=0.3, name="halve",
+            kept, swap(sent, "expert", step), vision_grad, far=(2,), cost=0.3, name="halve",
         )
         step *= 2
     finished = run(
         finish_kernel, shape((part, width)),
-        placed, text, kept, swap(sent, "expert", step), *vision, cost=1.0, name="finish",
+        placed, text, kept, swap(sent, "expert", step), *vision, sums_own, far=(4 + blocks,),
+        cost=1.0, name="finish",
     )
     laid = {0: finished}
     while step:

time: 151 us -> 124 us (0.82)
  local copies, waits for them, and re-layouts: 36 us -> 5.91 us
  waiting for transfers between devices: 43.5 us -> 47 us
    unnamed x66 -> x48, local copies, waits for them, and re-layouts: 36 us -> 5.91 us
    ppermute x38 -> x46, starting transfers between devices: 40.5 us -> 48.7 us  [swap(): return lax.ppermute(value, axis, [(i, i ^ step) for i in range(count)])]
    all_to_all x2 -> x0, starting transfers between devices: 7.23 us -> none  [send_all(): return lax.all_to_all(value, axis, split_axis=0, concat_axis=0, tiled=True)]
    ppermute x38 -> x46, waiting for transfers between devices: 43.5 us -> 47 us  [swap(): return lax.ppermute(value, axis, [(i, i ^ step) for i in range(count)])]
    pallas_call x1 -> x3, Pallas kernels: 2.45 us -> 0.01 us  [after(): pl.pallas_call(lambda *refs: None, out_shape=[shape(value.shape, value.dt...]
    pallas_call x18 -> x21, Pallas kernels: 18.9 us -> 20.9 us  [run(): pl.pallas_call(kernel, out_shape=outs, in_specs=specs, out_specs=jax.tree...]
  transfers between devices with their start and end apart: 40 -> 46, of which waited for: 18 -> 25; matrix products, arithmetic and copies ran while one was open for 0% -> 0% of each run, Pallas kernels for 7% -> 10%
where the time goes in v1:
time: 124 us
  starting transfers between devices  48.7 us (39%)
  waiting for transfers between devices  47 us (38%)
  Pallas kernels  21 us (17%)
  local copies, waits for them, and re-layouts  5.91 us (5%)
    ppermute x46, starting transfers between devices, swap(): return lax.ppermute(value, axis, [(i, i ^ step) for i in range(count)])  48.7 us
    ppermute x46, waiting for transfers between devices, swap(): return lax.ppermute(value, axis, [(i, i ^ step) for i in range(count)])  47 us
    pallas_call x21, Pallas kernels, run(): pl.pallas_call(kernel, out_shape=outs, in_specs=specs, out_specs=jax.tree...  20.9 us
    unnamed x48, local copies, waits for them, and re-layouts  5.91 us
  transfers between devices with their start and end apart: 46, of which 25 were waited for; matrix products, arithmetic and copies ran while one was open for 0% of the time, Pallas kernels for 10%

profile of v1, /device:TPU:0, one launch (start us, length us, event | category | flops | bytes accessed | tf_op | source)
XLA Modules:
  0.0 123.6 jit_solution(1134655378992298762)
XLA Ops:
  0.6 1.8 %pack.1.refs_3_ = bf16[592,128]{1,0:T(8,128)(2,1)} custom-call(bf16[288,128]{1,0:T(8,128)(2,1)} %bitcast.20, bf16[288,128]{1,0:T(8,128)(2,1)} %bitcast.21, s32[1,32]{1,0:T(1,128)} %bitcast.22, s32[1,32]{1,0:T(1,128)} %bitcast.23, s32[8,128]{1,0:T(8,128)} %bitcast.16), custom_call_target="tpu_custom_call" | custom-call | bytes 3000000 | tf_op jit(solution)/shard_map/pack/pallas_call | solution.py:514
  2.4 4.0 %collective-permute-start.3 = (bf16[592,128]{1,0:T(8,128)(2,1)}, bf16[592,128]{1,0:T(8,128)(2,1)S(1)}, u32[]{:S(2)}, u32[]{:S(2)}) collective-permute-start(bf16[592,128]{1,0:T(8,128)(2,1)} %pack.1.refs_3_), channel_id=1, source_target_pairs={{0,24},{4,28},{8,16},{12,20},{16,8},{20,12},{24,0},{28,4},{1,25},{... | collective-permute-start | bytes 454664 | tf_op jit(solution)/shard_map/ppermute | solution.py:560
  16.0 1.5 %collective-permute-start.7 = (bf16[48,2048]{1,0:T(8,128)(2,1)S(1)}, bf16[48,2048]{1,0:T(8,128)(2,1)S(1)}, u32[]{:S(2)}, u32[]{:S(2)}) collective-permute-start(bf16[48,2048]{1,0:T(8,128)(2,1)S(1)} %get-tuple-element.68), channel_id=1, source_target_pairs={{0,8},{4,12},{8,0},{12,4},{16,24},{20,28},{24,16},{28,20},{1,9},{5... | collective-permute-start | bytes 589832 | tf_op jit(solution)/shard_map/ppermute | solution.py:560
  19.5 5.8 %attend.1 = (bf16[32,1152]{1,0:T(8,128)(2,1)}, bf16[128,128]{1,0:T(8,128)(2,1)}, bf16[8,2432]{1,0:T(8,128)(2,1)}, bf16[8,2432]{1,0:T(8,128)(2,1)}, bf16[8,2432]{1,0:T(8,128)(2,1)}, /*index=5*/bf16[8,2432]{1,0:T(8,128)(2,1)}) custom-call(bf16[4,72,128]{2,1,0:T(8,128)(2,1)} %refs_0_.2, f32[4,288]{1,0:T(4,128)} %refs_0_.3, bf16[1152,2048]{1,0:T(8,128)(2,1)} %bitcast.9, ...), custom_call_target="tpu_custom_call" | custom-call | bytes 12000000 | tf_op jit(solution)/shard_map/attend/pallas_call | solution.py:514
  25.3 1.6 %collective-permute-start.10 = (bf16[8,2432]{1,0:T(8,128)(2,1)}, bf16[8,2432]{1,0:T(8,128)(2,1)S(1)}, u32[]{:S(2)}, u32[]{:S(2)}) collective-permute-start(bf16[8,2432]{1,0:T(8,128)(2,1)} %get-tuple-element.71), channel_id=1, source_target_pairs={{0,1},{1,0},{2,3},{3,2},{4,5},{5,4},{6,7},{7,6},{8,9},{9,8},{10,11... | collective-permute-start | bytes 116744 | tf_op jit(solution)/shard_map/ppermute | solution.py:560
  27.0 2.6 %collective-permute-start.11 = (bf16[8,2432]{1,0:T(8,128)(2,1)}, bf16[8,2432]{1,0:T(8,128)(2,1)S(1)}, u32[]{:S(2)}, u32[]{:S(2)}) collective-permute-start(bf16[8,2432]{1,0:T(8,128)(2,1)} %get-tuple-element.72), channel_id=1, source_target_pairs={{0,2},{1,3},{2,0},{3,1},{4,6},{5,7},{6,4},{7,5},{8,10},{9,11},{10,... | collective-permute-start | bytes 116744 | tf_op jit(solution)/shard_map/ppermute | solution.py:560
  29.6 3.6 %collective-permute-start.12 = (bf16[8,2432]{1,0:T(8,128)(2,1)}, bf16[8,2432]{1,0:T(8,128)(2,1)S(1)}, u32[]{:S(2)}, u32[]{:S(2)}) collective-permute-start(bf16[8,2432]{1,0:T(8,128)(2,1)} %get-tuple-element.73), channel_id=1, source_target_pairs={{0,3},{1,2},{2,1},{3,0},{4,7},{5,6},{6,5},{7,4},{8,11},{9,10},{10,... | collective-permute-start | bytes 116744 | tf_op jit(solution)/shard_map/ppermute | solution.py:560
  33.2 2.4 %collective-permute-done.12.refs_6_.refs_3_ = bf16[8,2432]{1,0:T(8,128)(2,1)S(1)} collective-permute-done((bf16[8,2432]{1,0:T(8,128)(2,1)}, bf16[8,2432]{1,0:T(8,128)(2,1)S(1)}, u32[]{:S(2)}, u32[]{:S(2)}) %collective-permute-start.12) | collective-permute-done | bytes 38944 | tf_op jit(solution)/shard_map/ppermute | solution.py:560
  36.8 3.7 %collective-permute-start.16 = (bf16[8,2176]{1,0:T(8,128)(2,1)S(1)}, bf16[8,2176]{1,0:T(8,128)(2,1)S(1)}, u32[]{:S(2)}, u32[]{:S(2)}) collective-permute-start(bf16[8,2176]{1,0:T(8,128)(2,1)S(1)} %merge.1.refs_0_.own_ref), channel_id=1, source_target_pairs={{0,3},{1,2},{2,1},{3,0},{4,7},{5,6},{6,5},{7,4},{8,11},{9,10},{10,... | collective-permute-start | bytes 104456 | tf_op jit(solution)/shard_map/ppermute | solution.py:560
  42.8 2.5 %collective-permute-done.15.refs_2_ = bf16[8,2176]{1,0:T(8,128)(2,1)S(1)} collective-permute-done((bf16[8,2176]{1,0:T(8,128)(2,1)S(1)}, bf16[8,2176]{1,0:T(8,128)(2,1)S(1)}, u32[]{:S(2)}, u32[]{:S(2)}) %collective-permute-start.15) | collective-permute-done | bytes 34848 | tf_op jit(solution)/shard_map/ppermute | solution.py:560
  45.4 1.7 %collective-permute-start.22 = (bf16[32,2176]{1,0:T(8,128)(2,1)S(1)}, bf16[32,2176]{1,0:T(8,128)(2,1)S(1)}, u32[]{:S(2)}, u32[]{:S(2)}) collective-permute-start(bf16[32,2176]{1,0:T(8,128)(2,1)S(1)} %stack.1.refs_6_.refs_2_.refs_0_.scalar_ref), channel_id=1, source_target_pairs={{0,24},{4,28},{8,16},{12,20},{16,8},{20,12},{24,0},{28,4},{1,25},{... | collective-permute-start | bytes 417800 | tf_op jit(solution)/shard_map/ppermute | solution.py:560
  48.9 3.6 %collective-permute-done.22.refs_12_.refs_6_ = bf16[32,2176]{1,0:T(8,128)(2,1)S(1)} collective-permute-done((bf16[32,2176]{1,0:T(8,128)(2,1)S(1)}, bf16[32,2176]{1,0:T(8,128)(2,1)S(1)}, u32[]{:S(2)}, u32[]{:S(2)}) %collective-permute-start.22) | collective-permute-done | bytes 139296 | tf_op jit(solution)/shard_map/ppermute | solution.py:560
  55.9 3.3 %forward.1 = (f32[128,768]{1,0:T(8,128)S(1)}, f32[128,768]{1,0:T(8,128)S(1)}, bf16[32,2048]{1,0:T(8,128)(2,1)S(1)}, bf16[32,2048]{1,0:T(8,128)(2,1)S(1)}, bf16[3...) custom-call(bf16[128,256]{1,0:T(8,128)(2,1)S(1)} %get-tuple-element.66.refs_0_.slots_ref, f32[1,2048]{1,0:T(1,128)S(1)} %bitcast.14, ...), custom_call_target="tpu_custom_call" | custom-call | bytes 12000000 | tf_op jit(solution)/shard_map/forward/pallas_call | solution.py:514
  60.7 2.1 %collective-permute-done.24.sibling_ref = bf16[160,2048]{1,0:T(8,128)(2,1)S(1)} collective-permute-done((bf16[160,2048]{1,0:T(8,128)(2,1)S(1)}, bf16[160,2048]{1,0:T(8,128)(2,1)S(1)}, u32[]{:S(2)}, u32[]{:S(2)}) %collective-permute-start.24) | collective-permute-done | bytes 655392 | tf_op jit(solution)/shard_map/ppermute | solution.py:560
  62.9 1.5 %collective-permute-start.25 = (bf16[40,2048]{1,0:T(8,128)(2,1)S(1)}, bf16[40,2048]{1,0:T(8,128)(2,1)S(1)}, u32[]{:S(2)}, u32[]{:S(2)}) collective-permute-start(bf16[40,2048]{1,0:T(8,128)(2,1)S(1)} %get-tuple-element.86), channel_id=1, source_target_pairs={{0,8},{4,12},{8,0},{12,4},{16,24},{20,28},{24,16},{28,20},{1,9},{5... | collective-permute-start | bytes 491528 | tf_op jit(solution)/shard_map/ppermute | solution.py:560
  66.5 3.6 %collective-permute-done.25.refs_4_.refs_1_ = bf16[40,2048]{1,0:T(8,128)(2,1)S(1)} collective-permute-done((bf16[40,2048]{1,0:T(8,128)(2,1)S(1)}, bf16[40,2048]{1,0:T(8,128)(2,1)S(1)}, u32[]{:S(2)}, u32[]{:S(2)}) %collective-permute-start.25) | collective-permute-done | bytes 163872 | tf_op jit(solution)/shard_map/ppermute | solution.py:560
  70.0 1.5 %collective-permute-start.26 = (bf16[32,2048]{1,0:T(8,128)(2,1)S(1)}, bf16[32,2048]{1,0:T(8,128)(2,1)S(1)}, u32[]{:S(2)}, u32[]{:S(2)}) collective-permute-start(bf16[32,2048]{1,0:T(8,128)(2,1)S(1)} %get-tuple-element.88), channel_id=1, source_target_pairs={{0,8},{4,12},{8,0},{12,4},{16,24},{20,28},{24,16},{28,20},{1,9},{5... | collective-permute-start | bytes 393224 | tf_op jit(solution)/shard_map/ppermute | solution.py:560
  74.5 1.9 %collective-permute-done.26.refs_1_ = bf16[32,2048]{1,0:T(8,128)(2,1)S(1)} collective-permute-done((bf16[32,2048]{1,0:T(8,128)(2,1)S(1)}, bf16[32,2048]{1,0:T(8,128)(2,1)S(1)}, u32[]{:S(2)}, u32[]{:S(2)}) %collective-permute-start.26) | collective-permute-done | bytes 131104 | tf_op jit(solution)/shard_map/ppermute | solution.py:560
  76.5 3.1 %collective-permute-done.27.refs_2_ = bf16[32,2048]{1,0:T(8,128)(2,1)S(1)} collective-permute-done((bf16[32,2048]{1,0:T(8,128)(2,1)S(1)}, bf16[32,2048]{1,0:T(8,128)(2,1)S(1)}, u32[]{:S(2)}, u32[]{:S(2)}) %collective-permute-start.27) | collective-permute-done | bytes 131104 | tf_op jit(solution)/shard_map/ppermute | solution.py:560
  79.7 1.5 %collective-permute-done.31.refs_4_ = bf16[64,2048]{1,0:T(8,128)(2,1)S(1)} collective-permute-done((bf16[64,2048]{1,0:T(8,128)(2,1)S(1)}, bf16[64,2048]{1,0:T(8,128)(2,1)S(1)}, u32[]{:S(2)}, u32[]{:S(2)}) %collective-permute-start.31) | collective-permute-done | bytes 262176 | tf_op jit(solution)/shard_map/ppermute | solution.py:560
  83.8 2.0 %collective-permute-start.34 = (bf16[8,2048]{1,0:T(8,128)(2,1)S(1)}, bf16[8,2048]{1,0:T(8,128)(2,1)S(1)}, u32[]{:S(2)}, u32[]{:S(2)}) collective-permute-start(bf16[8,2048]{1,0:T(8,128)(2,1)S(1)} %get-tuple-element.99), channel_id=1, source_target_pairs={{0,2},{1,3},{2,0},{3,1},{4,6},{5,7},{6,4},{7,5},{8,10},{9,11},{10,... | collective-permute-start | bytes 98312 | tf_op jit(solution)/shard_map/ppermute | solution.py:560
  86.8 4.7 %collective-permute-done.33.refs_1_ = bf16[8,2048]{1,0:T(8,128)(2,1)S(1)} collective-permute-done((bf16[8,2048]{1,0:T(8,128)(2,1)S(1)}, bf16[8,2048]{1,0:T(8,128)(2,1)S(1)}, u32[]{:S(2)}, u32[]{:S(2)}) %collective-permute-start.33) | collective-permute-done | bytes 32800 | tf_op jit(solution)/shard_map/ppermute | solution.py:560
  91.5 2.1 %collective-permute-done.35.refs_3_ = bf16[8,2048]{1,0:T(8,128)(2,1)S(1)} collective-permute-done((bf16[8,2048]{1,0:T(8,128)(2,1)S(1)}, bf16[8,2048]{1,0:T(8,128)(2,1)S(1)}, u32[]{:S(2)}, u32[]{:S(2)}) %collective-permute-start.35) | collective-permute-done | bytes 32800 | tf_op jit(solution)/shard_map/ppermute | solution.py:560
  93.9 2.6 %collective-permute-start.39 = (bf16[8,2048]{1,0:T(8,128)(2,1)S(1)}, bf16[8,2048]{1,0:T(8,128)(2,1)S(1)}, u32[]{:S(2)}, u32[]{:S(2)}) collective-permute-start(bf16[8,2048]{1,0:T(8,128)(2,1)S(1)} %norm_grad.1._.refs_4_), channel_id=1, source_target_pairs={{0,3},{1,2},{2,1},{3,0},{4,7},{5,6},{6,5},{7,4},{8,11},{9,10},{10,... | collective-permute-start | bytes 98312 | tf_op jit(solution)/shard_map/ppermute | solution.py:560
  98.3 2.1 %collective-permute-done.39.refs_7_ = bf16[8,2048]{1,0:T(8,128)(2,1)S(1)} collective-permute-done((bf16[8,2048]{1,0:T(8,128)(2,1)S(1)}, bf16[8,2048]{1,0:T(8,128)(2,1)S(1)}, u32[]{:S(2)}, u32[]{:S(2)}) %collective-permute-start.39) | collective-permute-done | bytes 32800 | tf_op jit(solution)/shard_map/ppermute | solution.py:560
  100.5 3.7 %collective-permute-done.38.refs_6_ = bf16[8,2048]{1,0:T(8,128)(2,1)S(1)} collective-permute-done((bf16[8,2048]{1,0:T(8,128)(2,1)S(1)}, bf16[8,2048]{1,0:T(8,128)(2,1)S(1)}, u32[]{:S(2)}, u32[]{:S(2)}) %collective-permute-start.38) | collective-permute-done | bytes 32800 | tf_op jit(solution)/shard_map/ppermute | solution.py:560
  104.2 1.6 %merge_grad.1 = (f32[32,1152]{1,0:T(8,128)S(1)}, f32[32,128]{1,0:T(8,128)S(1)}) custom-call(f32[4,288]{1,0:T(4,128)S(1)} %copy-done.19, bf16[32,1152]{1,0:T(8,128)(2,1)S(1)} %copy-done.14, bf16[32,2176]{1,0:T(8,128)(2,1)S(1)} %stack.1.refs_6_.refs_2_.refs_0_.scalar_ref, bf16[1152,2048]{1,0:T(8,128)(2,1)S(1)} %bitcast.12, ...), custom_call_target="tpu_custom_call" | custom-call | bytes 7500000 | tf_op jit(solution)/shard_map/merge_grad/pallas_call | solution.py:514
  106.8 1.8 %collective-permute-start.40 = (bf16[32,2048]{1,0:T(8,128)(2,1)S(1)}, bf16[32,2048]{1,0:T(8,128)(2,1)S(1)}, u32[]{:S(2)}, u32[]{:S(2)}) collective-permute-start(bf16[32,2048]{1,0:T(8,128)(2,1)S(1)} %finish.1.refs_0_), channel_id=1, source_target_pairs={{0,1},{1,0},{2,3},{3,2},{4,5},{5,4},{6,7},{7,6},{8,9},{9,8},{10,11... | collective-permute-start | bytes 393224 | tf_op jit(solution)/shard_map/ppermute | solution.py:560
  108.6 5.4 %collective-permute-done.41.refs_2_ = bf16[32,2048]{1,0:T(8,128)(2,1)S(1)} collective-permute-done((bf16[32,2048]{1,0:T(8,128)(2,1)S(1)}, bf16[32,2048]{1,0:T(8,128)(2,1)S(1)}, u32[]{:S(2)}, u32[]{:S(2)}) %collective-permute-start.41) | collective-permute-done | bytes 131104 | tf_op jit(solution)/shard_map/ppermute | solution.py:560
  114.0 2.0 %collective-permute-start.45 = (f32[32,128]{1,0:T(8,128)S(1)}, f32[32,128]{1,0:T(8,128)S(1)}, u32[]{:S(2)}, u32[]{:S(2)}) collective-permute-start(f32[32,128]{1,0:T(8,128)S(1)} %get-tuple-element.104.refs_8_.refs_0_), channel_id=1, source_target_pairs={{0,3},{1,2},{2,1},{3,0},{4,7},{5,6},{6,5},{7,4},{8,11},{9,10},{10,... | collective-permute-start | bytes 49160 | tf_op jit(solution)/shard_map/ppermute | solution.py:560
  116.0 1.5 %collective-permute-start.44 = (f32[32,128]{1,0:T(8,128)S(1)}, f32[32,128]{1,0:T(8,128)S(1)}, u32[]{:S(2)}, u32[]{:S(2)}) collective-permute-start(f32[32,128]{1,0:T(8,128)S(1)} %get-tuple-element.104.refs_8_.refs_0_), channel_id=1, source_target_pairs={{0,2},{1,3},{2,0},{3,1},{4,6},{5,7},{6,4},{7,5},{8,10},{9,11},{10,... | collective-permute-start | bytes 49160 | tf_op jit(solution)/shard_map/ppermute | solution.py:560
  121.2 1.6 %unfold.1 = f32[288,128]{1,0:T(8,128)} custom-call(f32[32,1152]{1,0:T(8,128)S(1)} %get-tuple-element.105.grad_ref, bf16[32,1152]{1,0:T(8,128)(2,1)S(1)} %copy-done.14, bf16[32,2176]{1,0:T(8,128)(2,1)S(1)} %stack.1.refs_6_.refs_2_.refs_0_.scalar_ref, f32[32,128]{1,0:T(8,128)S(1)} %get-tuple-element.104.refs_8_.refs_0_, ...), custom_call_target="tpu_custom_call" | custom-call | bytes 6000000 | tf_op jit(solution)/shard_map/unfold/pallas_call | solution.py:514
  (133 shorter events, 38.2 us)
Async XLA Ops:
  2.4 10.0 %collective-permute-start.3 = (bf16[592,128]{1,0:T(8,128)(2,1)}, bf16[592,128]{1,0:T(8,128)(2,1)S(1)}, u32[]{:S(2)}, u32[]{:S(2)}) collective-permute-start(bf16[592,128]{1,0:T(8,128)(2,1)} %pack.1.refs_3_), channel_id=1, source_target_pairs={{0,24},{4,28},{8,16},{12,20},{16,8},{20,12},{24,0},{28,4},{1,25},{... | collective-permute-start | bytes 454664 | tf_op jit(solution)/shard_map/ppermute | solution.py:560
  6.4 7.4 %collective-permute-start.2 = (bf16[592,128]{1,0:T(8,128)(2,1)}, bf16[592,128]{1,0:T(8,128)(2,1)S(1)}, u32[]{:S(2)}, u32[]{:S(2)}) collective-permute-start(bf16[592,128]{1,0:T(8,128)(2,1)} %pack.1.refs_3_), channel_id=1, source_target_pairs={{0,16},{4,20},{8,24},{12,28},{16,0},{20,4},{24,8},{28,12},{1,17},{... | collective-permute-start | bytes 454664 | tf_op jit(solution)/shard_map/ppermute | solution.py:560
  6.9 7.2 %collective-permute-start.1 = (bf16[592,128]{1,0:T(8,128)(2,1)}, bf16[592,128]{1,0:T(8,128)(2,1)S(1)}, u32[]{:S(2)}, u32[]{:S(2)}) collective-permute-start(bf16[592,128]{1,0:T(8,128)(2,1)} %pack.1.refs_3_), channel_id=1, source_target_pairs={{0,8},{4,12},{8,0},{12,4},{16,24},{20,28},{24,16},{28,20},{1,9},{5... | collective-permute-start | bytes 454664 | tf_op jit(solution)/shard_map/ppermute | solution.py:560
  7.0 7.7 %collective-permute-start = (bf16[592,128]{1,0:T(8,128)(2,1)}, bf16[592,128]{1,0:T(8,128)(2,1)S(1)}, u32[]{:S(2)}, u32[]{:S(2)}) collective-permute-start(bf16[592,128]{1,0:T(8,128)(2,1)} %pack.1.refs_3_), channel_id=1, source_target_pairs={{0,4},{4,0},{8,12},{12,8},{16,20},{20,16},{24,28},{28,24},{1,5},{5... | collective-permute-start | bytes 454664 | tf_op jit(solution)/shard_map/ppermute | solution.py:560
  16.0 19.6 %collective-permute-start.7 = (bf16[48,2048]{1,0:T(8,128)(2,1)S(1)}, bf16[48,2048]{1,0:T(8,128)(2,1)S(1)}, u32[]{:S(2)}, u32[]{:S(2)}) collective-permute-start(bf16[48,2048]{1,0:T(8,128)(2,1)S(1)} %get-tuple-element.68), channel_id=1, source_target_pairs={{0,8},{4,12},{8,0},{12,4},{16,24},{20,28},{24,16},{28,20},{1,9},{5... | collective-permute-start | bytes 589832 | tf_op jit(solution)/shard_map/ppermute | solution.py:560
  17.5 18.1 %collective-permute-start.8 = (bf16[48,2048]{1,0:T(8,128)(2,1)S(1)}, bf16[48,2048]{1,0:T(8,128)(2,1)S(1)}, u32[]{:S(2)}, u32[]{:S(2)}) collective-permute-start(bf16[48,2048]{1,0:T(8,128)(2,1)S(1)} %get-tuple-element.69), channel_id=1, source_target_pairs={{0,16},{4,20},{8,24},{12,28},{16,0},{20,4},{24,8},{28,12},{1,17},{... | collective-permute-start | bytes 589832 | tf_op jit(solution)/shard_map/ppermute | solution.py:560
  18.1 17.5 %collective-permute-start.9 = (bf16[48,2048]{1,0:T(8,128)(2,1)S(1)}, bf16[48,2048]{1,0:T(8,128)(2,1)S(1)}, u32[]{:S(2)}, u32[]{:S(2)}) collective-permute-start(bf16[48,2048]{1,0:T(8,128)(2,1)S(1)} %get-tuple-element.70), channel_id=1, source_target_pairs={{0,24},{4,28},{8,16},{12,20},{16,8},{20,12},{24,0},{28,4},{1,25},{... | collective-permute-start | bytes 589832 | tf_op jit(solution)/shard_map/ppermute | solution.py:560
  27.0 6.2 %collective-permute-start.11 = (bf16[8,2432]{1,0:T(8,128)(2,1)}, bf16[8,2432]{1,0:T(8,128)(2,1)S(1)}, u32[]{:S(2)}, u32[]{:S(2)}) collective-permute-start(bf16[8,2432]{1,0:T(8,128)(2,1)} %get-tuple-element.72), channel_id=1, source_target_pairs={{0,2},{1,3},{2,0},{3,1},{4,6},{5,7},{6,4},{7,5},{8,10},{9,11},{10,... | collective-permute-start | bytes 116744 | tf_op jit(solution)/shard_map/ppermute | solution.py:560
  29.6 6.0 %collective-permute-start.12 = (bf16[8,2432]{1,0:T(8,128)(2,1)}, bf16[8,2432]{1,0:T(8,128)(2,1)S(1)}, u32[]{:S(2)}, u32[]{:S(2)}) collective-permute-start(bf16[8,2432]{1,0:T(8,128)(2,1)} %get-tuple-element.73), channel_id=1, source_target_pairs={{0,3},{1,2},{2,1},{3,0},{4,7},{5,6},{6,5},{7,4},{8,11},{9,10},{10,... | collective-permute-start | bytes 116744 | tf_op jit(solution)/shard_map/ppermute | solution.py:560
  35.7 5.6 %collective-permute-start.13 = (bf16[96,2048]{1,0:T(8,128)(2,1)S(1)}, bf16[96,2048]{1,0:T(8,128)(2,1)S(1)}, u32[]{:S(2)}, u32[]{:S(2)}) collective-permute-start(bf16[96,2048]{1,0:T(8,128)(2,1)S(1)} %early_half.1), channel_id=1, source_target_pairs={{0,4},{4,0},{8,12},{12,8},{16,20},{20,16},{24,28},{28,24},{1,5},{5... | collective-permute-start | bytes 1179656 | tf_op jit(solution)/shard_map/ppermute | solution.py:560
  36.8 6.0 %collective-permute-start.16 = (bf16[8,2176]{1,0:T(8,128)(2,1)S(1)}, bf16[8,2176]{1,0:T(8,128)(2,1)S(1)}, u32[]{:S(2)}, u32[]{:S(2)}) collective-permute-start(bf16[8,2176]{1,0:T(8,128)(2,1)S(1)} %merge.1.refs_0_.own_ref), channel_id=1, source_target_pairs={{0,3},{1,2},{2,1},{3,0},{4,7},{5,6},{6,5},{7,4},{8,11},{9,10},{10,... | collective-permute-start | bytes 104456 | tf_op jit(solution)/shard_map/ppermute | solution.py:560
  45.4 7.2 %collective-permute-start.22 = (bf16[32,2176]{1,0:T(8,128)(2,1)S(1)}, bf16[32,2176]{1,0:T(8,128)(2,1)S(1)}, u32[]{:S(2)}, u32[]{:S(2)}) collective-permute-start(bf16[32,2176]{1,0:T(8,128)(2,1)S(1)} %stack.1.refs_6_.refs_2_.refs_0_.scalar_ref), channel_id=1, source_target_pairs={{0,24},{4,28},{8,16},{12,20},{16,8},{20,12},{24,0},{28,4},{1,25},{... | collective-permute-start | bytes 417800 | tf_op jit(solution)/shard_map/ppermute | solution.py:560
  47.1 6.8 %collective-permute-start.20 = (bf16[32,2176]{1,0:T(8,128)(2,1)S(1)}, bf16[32,2176]{1,0:T(8,128)(2,1)S(1)}, u32[]{:S(2)}, u32[]{:S(2)}) collective-permute-start(bf16[32,2176]{1,0:T(8,128)(2,1)S(1)} %stack.1.refs_6_.refs_2_.refs_0_.scalar_ref), channel_id=1, source_target_pairs={{0,16},{4,20},{8,24},{12,28},{16,0},{20,4},{24,8},{28,12},{1,17},{... | collective-permute-start | bytes 417800 | tf_op jit(solution)/shard_map/ppermute | solution.py:560
  48.9 6.9 %collective-permute-start.17 = (bf16[32,2176]{1,0:T(8,128)(2,1)S(1)}, bf16[32,2176]{1,0:T(8,128)(2,1)S(1)}, u32[]{:S(2)}, u32[]{:S(2)}) collective-permute-start(bf16[32,2176]{1,0:T(8,128)(2,1)S(1)} %stack.1.refs_6_.refs_2_.refs_0_.scalar_ref), channel_id=1, source_target_pairs={{0,4},{4,0},{8,12},{12,8},{16,20},{20,16},{24,28},{28,24},{1,5},{5... | collective-permute-start | bytes 417800 | tf_op jit(solution)/shard_map/ppermute | solution.py:560
  62.9 7.1 %collective-permute-start.25 = (bf16[40,2048]{1,0:T(8,128)(2,1)S(1)}, bf16[40,2048]{1,0:T(8,128)(2,1)S(1)}, u32[]{:S(2)}, u32[]{:S(2)}) collective-permute-start(bf16[40,2048]{1,0:T(8,128)(2,1)S(1)} %get-tuple-element.86), channel_id=1, source_target_pairs={{0,8},{4,12},{8,0},{12,4},{16,24},{20,28},{24,16},{28,20},{1,9},{5... | collective-permute-start | bytes 491528 | tf_op jit(solution)/shard_map/ppermute | solution.py:560
  64.5 9.3 %collective-permute-start.29 = (bf16[40,2048]{1,0:T(8,128)(2,1)S(1)}, bf16[40,2048]{1,0:T(8,128)(2,1)S(1)}, u32[]{:S(2)}, u32[]{:S(2)}) collective-permute-start(bf16[40,2048]{1,0:T(8,128)(2,1)S(1)} %get-tuple-element.92), channel_id=1, source_target_pairs={{0,16},{4,20},{8,24},{12,28},{16,0},{20,4},{24,8},{28,12},{1,17},{... | collective-permute-start | bytes 491528 | tf_op jit(solution)/shard_map/ppermute | solution.py:560
  65.2 9.2 %collective-permute-start.30 = (bf16[40,2048]{1,0:T(8,128)(2,1)S(1)}, bf16[40,2048]{1,0:T(8,128)(2,1)S(1)}, u32[]{:S(2)}, u32[]{:S(2)}) collective-permute-start(bf16[40,2048]{1,0:T(8,128)(2,1)S(1)} %get-tuple-element.93), channel_id=1, source_target_pairs={{0,24},{4,28},{8,16},{12,20},{16,8},{20,12},{24,0},{28,4},{1,25},{... | collective-permute-start | bytes 491528 | tf_op jit(solution)/shard_map/ppermute | solution.py:560
  70.0 6.4 %collective-permute-start.26 = (bf16[32,2048]{1,0:T(8,128)(2,1)S(1)}, bf16[32,2048]{1,0:T(8,128)(2,1)S(1)}, u32[]{:S(2)}, u32[]{:S(2)}) collective-permute-start(bf16[32,2048]{1,0:T(8,128)(2,1)S(1)} %get-tuple-element.88), channel_id=1, source_target_pairs={{0,8},{4,12},{8,0},{12,4},{16,24},{20,28},{24,16},{28,20},{1,9},{5... | collective-permute-start | bytes 393224 | tf_op jit(solution)/shard_map/ppermute | solution.py:560
  71.5 8.0 %collective-permute-start.27 = (bf16[32,2048]{1,0:T(8,128)(2,1)S(1)}, bf16[32,2048]{1,0:T(8,128)(2,1)S(1)}, u32[]{:S(2)}, u32[]{:S(2)}) collective-permute-start(bf16[32,2048]{1,0:T(8,128)(2,1)S(1)} %get-tuple-element.89), channel_id=1, source_target_pairs={{0,16},{4,20},{8,24},{12,28},{16,0},{20,4},{24,8},{28,12},{1,17},{... | collective-permute-start | bytes 393224 | tf_op jit(solution)/shard_map/ppermute | solution.py:560
  72.3 7.3 %collective-permute-start.28 = (bf16[32,2048]{1,0:T(8,128)(2,1)S(1)}, bf16[32,2048]{1,0:T(8,128)(2,1)S(1)}, u32[]{:S(2)}, u32[]{:S(2)}) collective-permute-start(bf16[32,2048]{1,0:T(8,128)(2,1)S(1)} %get-tuple-element.90), channel_id=1, source_target_pairs={{0,24},{4,28},{8,16},{12,20},{16,8},{20,12},{24,0},{28,4},{1,25},{... | collective-permute-start | bytes 393224 | tf_op jit(solution)/shard_map/ppermute | solution.py:560
  81.7 12.1 %collective-permute-start.32 = (bf16[64,2048]{1,0:T(8,128)(2,1)S(1)}, bf16[64,2048]{1,0:T(8,128)(2,1)S(1)}, u32[]{:S(2)}, u32[]{:S(2)}) collective-permute-start(bf16[64,2048]{1,0:T(8,128)(2,1)S(1)} %get-tuple-element.96), channel_id=1, source_target_pairs={{0,1},{1,0},{2,3},{3,2},{4,5},{5,4},{6,7},{7,6},{8,9},{9,8},{10,11... | collective-permute-start | bytes 786440 | tf_op jit(solution)/shard_map/ppermute | solution.py:560
  82.4 9.1 %collective-permute-start.33 = (bf16[8,2048]{1,0:T(8,128)(2,1)S(1)}, bf16[8,2048]{1,0:T(8,128)(2,1)S(1)}, u32[]{:S(2)}, u32[]{:S(2)}) collective-permute-start(bf16[8,2048]{1,0:T(8,128)(2,1)S(1)} %get-tuple-element.98), channel_id=1, source_target_pairs={{0,1},{1,0},{2,3},{3,2},{4,5},{5,4},{6,7},{7,6},{8,9},{9,8},{10,11... | collective-permute-start | bytes 98312 | tf_op jit(solution)/shard_map/ppermute | solution.py:560
  83.8 7.7 %collective-permute-start.34 = (bf16[8,2048]{1,0:T(8,128)(2,1)S(1)}, bf16[8,2048]{1,0:T(8,128)(2,1)S(1)}, u32[]{:S(2)}, u32[]{:S(2)}) collective-permute-start(bf16[8,2048]{1,0:T(8,128)(2,1)S(1)} %get-tuple-element.99), channel_id=1, source_target_pairs={{0,2},{1,3},{2,0},{3,1},{4,6},{5,7},{6,4},{7,5},{8,10},{9,11},{10,... | collective-permute-start | bytes 98312 | tf_op jit(solution)/shard_map/ppermute | solution.py:560
  85.8 7.9 %collective-permute-start.35 = (bf16[8,2048]{1,0:T(8,128)(2,1)S(1)}, bf16[8,2048]{1,0:T(8,128)(2,1)S(1)}, u32[]{:S(2)}, u32[]{:S(2)}) collective-permute-start(bf16[8,2048]{1,0:T(8,128)(2,1)S(1)} %get-tuple-element.100), channel_id=1, source_target_pairs={{0,3},{1,2},{2,1},{3,0},{4,7},{5,6},{6,5},{7,4},{8,11},{9,10},{10,... | collective-permute-start | bytes 98312 | tf_op jit(solution)/shard_map/ppermute | solution.py:560
  93.8 11.9 %collective-permute-start.36 = (bf16[32,2048]{1,0:T(8,128)(2,1)S(1)}, bf16[32,2048]{1,0:T(8,128)(2,1)S(1)}, u32[]{:S(2)}, u32[]{:S(2)}) collective-permute-start(bf16[32,2048]{1,0:T(8,128)(2,1)S(1)} %get-tuple-element.102), channel_id=1, source_target_pairs={{0,2},{1,3},{2,0},{3,1},{4,6},{5,7},{6,4},{7,5},{8,10},{9,11},{10,... | collective-permute-start | bytes 393224 | tf_op jit(solution)/shard_map/ppermute | solution.py:560
  93.9 6.6 %collective-permute-start.39 = (bf16[8,2048]{1,0:T(8,128)(2,1)S(1)}, bf16[8,2048]{1,0:T(8,128)(2,1)S(1)}, u32[]{:S(2)}, u32[]{:S(2)}) collective-permute-start(bf16[8,2048]{1,0:T(8,128)(2,1)S(1)} %norm_grad.1._.refs_4_), channel_id=1, source_target_pairs={{0,3},{1,2},{2,1},{3,0},{4,7},{5,6},{6,5},{7,4},{8,11},{9,10},{10,... | collective-permute-start | bytes 98312 | tf_op jit(solution)/shard_map/ppermute | solution.py:560
  96.5 7.7 %collective-permute-start.38 = (bf16[8,2048]{1,0:T(8,128)(2,1)S(1)}, bf16[8,2048]{1,0:T(8,128)(2,1)S(1)}, u32[]{:S(2)}, u32[]{:S(2)}) collective-permute-start(bf16[8,2048]{1,0:T(8,128)(2,1)S(1)} %norm_grad.1._.refs_4_), channel_id=1, source_target_pairs={{0,2},{1,3},{2,0},{3,1},{4,6},{5,7},{6,4},{7,5},{8,10},{9,11},{10,... | collective-permute-start | bytes 98312 | tf_op jit(solution)/shard_map/ppermute | solution.py:560
  96.9 7.2 %collective-permute-start.37 = (bf16[8,2048]{1,0:T(8,128)(2,1)S(1)}, bf16[8,2048]{1,0:T(8,128)(2,1)S(1)}, u32[]{:S(2)}, u32[]{:S(2)}) collective-permute-start(bf16[8,2048]{1,0:T(8,128)(2,1)S(1)} %norm_grad.1._.refs_4_), channel_id=1, source_target_pairs={{0,1},{1,0},{2,3},{3,2},{4,5},{5,4},{6,7},{7,6},{8,9},{9,8},{10,11... | collective-permute-start | bytes 98312 | tf_op jit(solution)/shard_map/ppermute | solution.py:560
  106.2 7.7 %collective-permute-start.41 = (bf16[32,2048]{1,0:T(8,128)(2,1)S(1)}, bf16[32,2048]{1,0:T(8,128)(2,1)S(1)}, u32[]{:S(2)}, u32[]{:S(2)}) collective-permute-start(bf16[32,2048]{1,0:T(8,128)(2,1)S(1)} %finish.1.refs_0_), channel_id=1, source_target_pairs={{0,2},{1,3},{2,0},{3,1},{4,6},{5,7},{6,4},{7,5},{8,10},{9,11},{10,... | collective-permute-start | bytes 393224 | tf_op jit(solution)/shard_map/ppermute | solution.py:560
  106.8 16.0 %collective-permute-start.40 = (bf16[32,2048]{1,0:T(8,128)(2,1)S(1)}, bf16[32,2048]{1,0:T(8,128)(2,1)S(1)}, u32[]{:S(2)}, u32[]{:S(2)}) collective-permute-start(bf16[32,2048]{1,0:T(8,128)(2,1)S(1)} %finish.1.refs_0_), channel_id=1, source_target_pairs={{0,1},{1,0},{2,3},{3,2},{4,5},{5,4},{6,7},{7,6},{8,9},{9,8},{10,11... | collective-permute-start | bytes 393224 | tf_op jit(solution)/shard_map/ppermute | solution.py:560
  114.0 8.8 %collective-permute-start.42 = (bf16[32,2048]{1,0:T(8,128)(2,1)S(1)}, bf16[32,2048]{1,0:T(8,128)(2,1)S(1)}, u32[]{:S(2)}, u32[]{:S(2)}) collective-permute-start(bf16[32,2048]{1,0:T(8,128)(2,1)S(1)} %collective-permute-done.41.refs_2_), channel_id=1, source_target_pairs={{0,1},{1,0},{2,3},{3,2},{4,5},{5,4},{6,7},{7,6},{8,9},{9,8},{10,11... | collective-permute-start | bytes 393224 | tf_op jit(solution)/shard_map/ppermute | solution.py:560
  114.0 5.7 %collective-permute-start.45 = (f32[32,128]{1,0:T(8,128)S(1)}, f32[32,128]{1,0:T(8,128)S(1)}, u32[]{:S(2)}, u32[]{:S(2)}) collective-permute-start(f32[32,128]{1,0:T(8,128)S(1)} %get-tuple-element.104.refs_8_.refs_0_), channel_id=1, source_target_pairs={{0,3},{1,2},{2,1},{3,0},{4,7},{5,6},{6,5},{7,4},{8,11},{9,10},{10,... | collective-permute-start | bytes 49160 | tf_op jit(solution)/shard_map/ppermute | solution.py:560
  (38 other events, 383.6 us)
